TPU v7x, 32 devices: a whole 2x2x4 slice. The times are simulated.
32 devices in a mesh: space: 16 (over z, y, core), coil: 2 (over x).
Axes of the slice: x: 2, y: 2, z: 4, core: 2. Of those that a mesh axis runs over, the one named last changes fastest.
Arguments:
- spatial_coef: bfloat16 [16, 128, 128, 2, 128], P('coil', 'space'), may hold values from -6 to 6
- temporal_basis: bfloat16 [2, 16, 4], replicated, may hold values from -1.5 to 1.5
- coil_maps: bfloat16 [8, 128, 128, 2, 128], P('coil', 'space'), may hold values from -6 to 6
- field_steps: int32 [128, 128, 128], P('space'), may hold values from 0 to 255
- kspace_data: bfloat16 [8, 4, 128, 128, 2, 128], P('coil', None, None, 'space'), may hold values from -6 to 6
- sample_mask: int32 [4, 128, 128], P(None, 'space'), may hold values 0 or 1
Outputs:
- gradient: float32 [16, 128, 128, 2, 128], P('coil', 'space')
Inputs may be any that keep to these rules, and one draw needn't show every extreme that they name: `sample_mask`: 1 where a phase-encoding line is sampled at that point, else 0.
All inputs are finite; a program needn't handle non-finite values. No bound on the sum of `sample_mask` on one device may be relied on, other than what follows from the above.
Results may differ from a plain program's by a relative error of at most 0.014.
Values may be sent and summed in bfloat16 or wider, within the bound.
No kernel may reach another device: no remote copies, remote signals or barrier semaphores. Data moves between devices by JAX's collectives and lax.ppermute only.
A program may use at most 128 MiB of HBM per device.

v0:
```python
import functools
import math

import jax
import jax.numpy as jnp
import ml_dtypes
import numpy as np
from jax import lax
from jax.experimental import pallas as pl
from jax.experimental.pallas import tpu as pltpu
from jax.sharding import PartitionSpec as P

STEPS_CYCLE = 256
SENT_SIXTEENTHS = 9
PLANES = 4
BACK_PLANES = 8
SOURCES = 8
HEAD = 2
UNROLL = 2
GRADIENT_PLANES = 2
VMEM_BYTES = 24 * 2**20
F32 = jnp.float32
BF16 = jnp.bfloat16


def real_table(length, sign, out_interleaved=False):
    index = np.arange(length)
    angle = (index[:, None] * index[None, :] % length) * (2.0 * math.pi / length)
    cosine = np.cos(angle) / math.sqrt(length)
    sine = sign * np.sin(angle) / math.sqrt(length)
    table = np.block([[cosine, -sine], [sine, cosine]])
    if out_interleaved:
        table = table.reshape(2, length, 2 * length).swapaxes(0, 1).reshape(2 * length, 2 * length)
    return jnp.asarray(table.astype(np.float32).astype(ml_dtypes.bfloat16))


def params():
    return pltpu.CompilerParams(vmem_limit_bytes=VMEM_BYTES)


def cost(flops, moved):
    return pl.CostEstimate(flops=int(flops), bytes_accessed=int(moved), transcendentals=0)


def whole_block(shape):
    return pl.BlockSpec(shape, lambda *_: (0,) * len(shape))


def unit_turn(steps):
    x = ((steps & (STEPS_CYCLE - 1)) - STEPS_CYCLE // 2).astype(F32) * (2.0 * math.pi / STEPS_CYCLE)
    square = x * x
    cosine = jnp.zeros_like(x)
    sine = jnp.zeros_like(x)
    for k in range(9, -1, -1):
        cosine = cosine * square + (-1.0) ** k / math.factorial(2 * k)
        sine = sine * square + (-1.0) ** k / math.factorial(2 * k + 1)
    return -cosine, -sine * x


def mix_factors(basis, block, interleaved):
    real, imaginary = basis[0], basis[1]
    eye = jnp.eye(block, dtype=basis.dtype)
    forward = jnp.stack([jnp.stack([real, -imaginary]), jnp.stack([imaginary, real])])
    adjoint = jnp.stack([jnp.stack([real, imaginary]), jnp.stack([-imaginary, real])])
    ranks, points = real.shape
    if interleaved:
        return jnp.einsum("qplt,yz->lyqtpz", adjoint, eye).reshape(
            ranks * block * 2, points * 2 * block
        )
    return jnp.einsum("qplt,yz->tqylzp", forward, eye).reshape(
        points * 2 * block, ranks * block * 2
    )


def image_kernel(points, block, mix_ref, order_ref, coef_ref, steps_ref, maps_ref, *rest):
    turned_refs, phase_refs = rest[:points], rest[points : 2 * points]
    planes_ref, mixed = rest[2 * points :]
    ranks, planes, rows2, depth = coef_ref.shape
    coils = maps_ref.shape[0]
    rows = rows2 // 2
    blocks = rows // block
    @pl.loop(0, planes, unroll=math.gcd(planes, UNROLL))
    def one(x):
        pair = 2 if blocks % 2 == 0 else 1
        for i in range(0, blocks, pair):
            columns = [
                jnp.concatenate(
                    [coef_ref[l, x, 2 * block * k : 2 * block * (k + 1), :] for l in range(ranks)],
                    axis=0,
                )
                for k in range(i, i + pair)
            ]
            image = jnp.dot(
                mix_ref[...], jnp.concatenate(columns, axis=1), preferred_element_type=F32
            )
            for k in range(pair):
                for j in range(2 * points):
                    mixed[j, (i + k) * block : (i + k + 1) * block, :] = image[
                        j * block : (j + 1) * block, k * depth : (k + 1) * depth
                    ]
        cosine, sine = unit_turn(steps_ref[x])
        now_cosine, now_sine = cosine, sine
        for t in range(points):
            if t:
                now_cosine, now_sine = (
                    now_cosine * cosine - now_sine * sine,
                    now_sine * cosine + now_cosine * sine,
                )
            real, imaginary = mixed[2 * t], mixed[2 * t + 1]
            turned_refs[t][x, 0] = (now_cosine * real - now_sine * imaginary).astype(BF16)
            turned_refs[t][x, 1] = (now_sine * real + now_cosine * imaginary).astype(BF16)
            phase_refs[t][x, 0] = now_cosine
            phase_refs[t][x, 1] = now_sine
        pair = 2 if coils % 2 == 0 else 1
        for c in range(0, coils, pair):
            both = jnp.concatenate([maps_ref[c + k, x] for k in range(pair)], axis=1)
            parted = jnp.dot(order_ref[...], both, preferred_element_type=F32).astype(BF16)
            for k in range(pair):
                planes_ref[c + k, x] = parted[:, k * depth : (k + 1) * depth].reshape(
                    2, rows, depth
                )


def make_images(mix, coef, steps, maps, points):
    ranks, slab, rows, depth = coef.shape
    coils = maps.shape[0]
    step = math.gcd(slab, PLANES)
    plane = (2, rows // 2, depth)
    plane_block = pl.BlockSpec((step,) + plane, lambda x: (x, 0, 0, 0))
    order = np.eye(rows, dtype=np.float32).reshape(rows // 2, 2, rows).swapaxes(0, 1)
    order = jnp.asarray(order.reshape(rows, rows).astype(ml_dtypes.bfloat16))
    outs = pl.pallas_call(
        functools.partial(image_kernel, points, mix.shape[0] // (2 * points)),
        grid=(slab // step,),
        in_specs=[
            whole_block(mix.shape),
            whole_block(order.shape),
            pl.BlockSpec((ranks, step, rows, depth), lambda x: (0, x, 0, 0)),
            pl.BlockSpec((step, rows // 2, depth), lambda x: (x, 0, 0)),
            pl.BlockSpec((coils, step, rows, depth), lambda x: (0, x, 0, 0)),
        ],
        out_specs=[plane_block] * (2 * points)
        + [pl.BlockSpec((coils, step) + plane, lambda x: (0, x, 0, 0, 0))],
        out_shape=[jax.ShapeDtypeStruct((slab,) + plane, BF16)] * points
        + [jax.ShapeDtypeStruct((slab,) + plane, F32)] * points
        + [jax.ShapeDtypeStruct((coils, slab) + plane, BF16)],
        scratch_shapes=[pltpu.VMEM((2 * points, rows // 2, depth), F32)],
        compiler_params=params(),
        cost_estimate=cost(4e9, 16e6),
        name="images",
    )(mix, order, coef, steps, maps)
    return outs[:points], outs[points : 2 * points], outs[2 * points]


def rank_kernel(slots, mask_ref, place_ref, plane_ref, base_ref):
    sources, points, slab_rows, depth = mask_ref.shape
    rows = sources * slab_rows
    before = lax.broadcasted_iota(jnp.int32, (depth, depth), 0) < lax.broadcasted_iota(
        jnp.int32, (depth, depth), 1
    )
    above = lax.broadcasted_iota(jnp.int32, (rows, rows), 0)
    left = lax.broadcasted_iota(jnp.int32, (rows, rows), 1)
    same = left // slab_rows == above // slab_rows
    lower = ((left < above) & same).astype(BF16)
    upper = ((above < left) & same).astype(BF16)
    for t in range(points):
        mask = mask_ref[:, t].astype(F32).reshape(rows, depth)
        packed = mask.astype(BF16)
        within = jnp.dot(packed, before.astype(BF16), preferred_element_type=F32)
        totals = jnp.dot(packed, jnp.ones((depth, depth), BF16), preferred_element_type=F32)
        starts = jnp.dot(lower, totals.astype(BF16), preferred_element_type=F32)
        rank = within + starts
        place = rank - jnp.floor(rank * (1.0 / depth)) * depth
        place_ref[t] = jnp.where((mask > 0.0) & (rank < slots), place, -1.0)
        plane_ref[t] = packed
        across = lax.dot_general(
            jnp.ones((8, depth), BF16), packed, (((1,), (1,)), ((), ())), preferred_element_type=F32
        )
        base_ref[t] = jnp.dot(across.astype(BF16), upper, preferred_element_type=F32).astype(
            jnp.int32
        )


def rank_cells(mask_all, slots):
    sources, points, slab_rows, depth = mask_all.shape
    rows = sources * slab_rows
    return pl.pallas_call(
        functools.partial(rank_kernel, slots),
        out_shape=[
            jax.ShapeDtypeStruct((points, rows, depth), F32),
            jax.ShapeDtypeStruct((points, rows, depth), BF16),
            jax.ShapeDtypeStruct((points, 8, rows), jnp.int32),
        ],
        compiler_params=params(),
        cost_estimate=cost(1e8, 1e6),
        name="ranks",
    )(mask_all)


def data_kernel(full, shared, split, extra, table_ref, mask_ref, extra_ref, data_ref, *rest):
    main_ref, last_ref = rest[0], rest[1] if split else None
    chosen, kept_shared = rest[-2:]
    slab_rows, depth = mask_ref.shape[1:]
    together = data_ref.shape[0]
    dests, held, _ = main_ref.shape
    width = extra_ref.shape[1]
    tiles = full + shared
    t, group = pl.program_id(0), pl.program_id(1)
    coils = together * pl.num_programs(1)
    units = coils * full + (coils // 2) * shared

    @pl.when(group == 0)
    def choose():
        mask = mask_ref[0]
        before = lax.broadcasted_iota(jnp.int32, (depth, depth), 0) < lax.broadcasted_iota(
            jnp.int32, (depth, depth), 1
        )
        within = jnp.dot(mask, before.astype(BF16), preferred_element_type=F32)
        totals = jnp.dot(mask, jnp.ones((depth, depth), BF16), preferred_element_type=F32)
        slot = lax.broadcasted_iota(jnp.int32, (full * depth, depth), 0).astype(F32)
        side = lax.broadcasted_iota(jnp.int32, (depth, depth), 0)
        left = jnp.where(side < depth // 2, side + full * depth, -2).astype(F32)
        right = jnp.where(side < depth // 2, -2, side + full * depth - depth // 2).astype(F32)
        start = jnp.zeros((1, depth), F32)
        wide = mask.astype(F32)
        for k in range(slab_rows):
            rank = jnp.where(wide[k : k + 1] > 0.0, within[k : k + 1] + start, -1.0)
            at = slice(k * depth, (k + 1) * depth)
            chosen[: full * depth, at] = jnp.where(slot == rank, 1.0, 0.0).astype(BF16)
            if shared:
                chosen[full * depth : (full + 1) * depth, at] = jnp.where(
                    left == rank, 1.0, 0.0
                ).astype(BF16)
                chosen[(full + 1) * depth :, at] = jnp.where(right == rank, 1.0, 0.0).astype(BF16)
            start = start + totals[k : k + 1]
        for e in range(extra):
            main_ref[:, held - (extra - e) * width : held - (extra - e - 1) * width] = (
                jnp.broadcast_to(extra_ref[e][None], (dests, width, depth))
            )

    parts = []
    for c in range(together):
        data = jnp.swapaxes(data_ref[c, 0], 0, 1)
        cells = jnp.concatenate(
            [jnp.concatenate([data[2 * k], data[2 * k + 1]], axis=0) for k in range(slab_rows)],
            axis=1,
        )
        by_slot = (((1,), (1,)), ((), ()))
        kept = lax.dot_general(
            cells, chosen[: full * depth], by_slot, preferred_element_type=F32
        ).astype(BF16)
        if shared:
            end = chosen[(full + c) * depth : (full + c + 1) * depth]
            last = lax.dot_general(cells, end, by_slot, preferred_element_type=F32).astype(BF16)
            kept = jnp.concatenate([kept, last], axis=1)
        turned = jnp.dot(table_ref[...], kept, preferred_element_type=F32)
        parts.append(
            [
                turned[:, i * depth : (i + 1) * depth].reshape(dests, width, depth)
                for i in range(tiles)
            ]
        )
    if shared:
        parts.append([parts[0].pop() + parts[1].pop()])

    def put(ref, unit, value):
        start = pl.multiple_of(unit * width, width)
        ref[:, pl.ds(start, width)] = value.astype(BF16)

    @pl.when(t < pl.num_programs(0) - (1 if split else 0))
    def whole():
        for c in range(together):
            for i in range(full):
                put(main_ref, t * units + (group * together + c) * full + i, parts[c][i])
        if shared:
            put(main_ref, t * units + coils * full + group, parts[-1][0])

    if split:

        @pl.when(t == pl.num_programs(0) - 1)
        def halves():
            half = width // 2
            for ref, base, at in (
                (main_ref, t * units, slice(0, half)),
                (last_ref, 0, slice(half, width)),
            ):
                for i in range(full):
                    both = jnp.concatenate([parts[c][i][:, at] for c in range(2)], axis=1)
                    put(ref, base + group * full + i, both)
            if shared:
                kept_shared[group % 2] = parts[-1][0]

                @pl.when(group % 2 == 1)
                def pairs():
                    for ref, base, at in (
                        (main_ref, t * units, slice(0, half)),
                        (last_ref, 0, slice(half, width)),
                    ):
                        both = jnp.concatenate([kept_shared[p][:, at] for p in range(2)], axis=1)
                        put(ref, base + (coils // 2) * full + group // 2, both)


def transform_data(table, mask, extra, data, start, count, dests, fit, split):
    coils, points, first, rows2, depth = data.shape
    width = 2 * first // dests
    full, shared = fit
    together = 2 if coils % 2 == 0 else 1
    units = coils * full + (coils // 2) * shared
    more = 0 if start else extra.shape[0]
    held = [units * count - (units // 2 if split else 0) + more] + [units // 2] * split
    return pl.pallas_call(
        functools.partial(data_kernel, full, shared, split, more),
        grid=(count, coils // together),
        in_specs=[
            whole_block(table.shape),
            pl.BlockSpec((1, rows2 // 2, depth), lambda t, c: (start + t, 0, 0)),
            whole_block(extra.shape),
            pl.BlockSpec((together, 1, first, rows2, depth), lambda t, c: (c, start + t, 0, 0, 0)),
        ],
        out_specs=[whole_block((dests, n * width, depth)) for n in held],
        out_shape=[jax.ShapeDtypeStruct((dests, n * width, depth), BF16) for n in held],
        scratch_shapes=[
            pltpu.VMEM(((full + 2 * shared) * depth, rows2 // 2 * depth), BF16),
            pltpu.VMEM((2, dests, width, depth), F32),
        ],
        compiler_params=pltpu.CompilerParams(vmem_limit_bytes=56 * 2**20),
        cost_estimate=cost(2e9 * count, 8e6 * count),
        name="data",
    )(table, mask, extra, data)


def forward_kernel(depth_ref, row_ref, own_ref, far_ref, maps_ref, out_ref):
    coils, planes, _, rows, depth = maps_ref.shape
    pair = 2 if coils % 2 == 0 else 1
    @pl.loop(0, planes, unroll=math.gcd(planes, UNROLL))
    def one(x):
        real = own_ref[x, 0].astype(F32) + far_ref[x, 0].astype(F32)
        imaginary = own_ref[x, 1].astype(F32) + far_ref[x, 1].astype(F32)
        for c in range(0, coils, pair):
            stacked = []
            for k in range(c, c + pair):
                map_real = maps_ref[k, x, 0].astype(F32)
                map_imaginary = maps_ref[k, x, 1].astype(F32)
                coil_real = (map_real * real - map_imaginary * imaginary).astype(BF16)
                coil_imaginary = (map_real * imaginary + map_imaginary * real).astype(BF16)
                stacked.append(jnp.concatenate([coil_real, coil_imaginary], axis=1))
            deep = jnp.dot(
                jnp.concatenate(stacked, axis=0), depth_ref[...], preferred_element_type=F32
            ).astype(BF16)
            columns = [
                jnp.concatenate(
                    [
                        deep[k * rows : (k + 1) * rows, :depth],
                        deep[k * rows : (k + 1) * rows, depth:],
                    ],
                    axis=0,
                )
                for k in range(pair)
            ]
            lines = jnp.dot(
                row_ref[...], jnp.concatenate(columns, axis=1), preferred_element_type=F32
            )
            for k in range(pair):
                out_ref[c + k, x] = lines[:, k * depth : (k + 1) * depth].astype(BF16)


def forward_lines(depth_table, row_table, own, far, maps):
    coils, slab, _, rows, depth = maps.shape
    step = math.gcd(slab, PLANES)
    plane_block = pl.BlockSpec((step, 2, rows, depth), lambda x: (x, 0, 0, 0))
    return pl.pallas_call(
        forward_kernel,
        grid=(slab // step,),
        in_specs=[
            whole_block(depth_table.shape),
            whole_block(row_table.shape),
            plane_block,
            plane_block,
            pl.BlockSpec((coils, step, 2, rows, depth), lambda x: (0, x, 0, 0, 0)),
        ],
        out_specs=pl.BlockSpec((coils, step, 2 * rows, depth), lambda x: (0, x, 0, 0)),
        out_shape=jax.ShapeDtypeStruct((coils, slab, 2 * rows, depth), BF16),
        compiler_params=params(),
        cost_estimate=cost(3e9, 8e6),
        name="forward",
    )(depth_table, row_table, own, far, maps)


def back_kernel(
    spreads, fit, halved, depth_ref, row_ref, base_ref, place_ref, mask_ref, data_ref, lines_ref,
    maps_ref, phase_ref, out_ref, held, ready
):
    coils, planes = maps_ref.shape[:2]
    rows, depth = maps_ref.shape[3:]
    sources = data_ref.shape[0]
    full, shared = fit
    tiles = full + shared
    width = ready.shape[3]
    unit = 2 * width if halved else width
    high = coils * width
    step = pl.program_id(0)
    slab_rows = rows // (spreads * sources)

    def piece(s, u, part):
        value = data_ref[s, u * unit : (u + 1) * unit].astype(F32)
        return value[part * width : (part + 1) * width] if halved else value

    @pl.when(step < spreads)
    def spread():
        lane = lax.broadcasted_iota(jnp.int32, (high, depth), 1)
        slot = lax.broadcasted_iota(jnp.int32, (depth, depth), 0).astype(F32)
        @pl.loop(0, sources, unroll=math.gcd(sources, UNROLL))
        def one(s):
            for c in range(coils):
                for i in range(full):
                    if halved:
                        ready[s % 2, c, i] = piece(s, (c // 2) * full + i, c % 2)
                    else:
                        ready[s % 2, c, i] = piece(s, c * full + i, 0)
                if shared:
                    if halved:
                        last = piece(s, (coils // 2) * full + c // 4, (c // 2) % 2)
                    else:
                        last = piece(s, coils * full + c // 2, 0)
                    ready[s % 2, c, full] = pltpu.roll(last, depth // 2, 1) if c % 2 else last
            first = pl.multiple_of((step * sources + s) * slab_rows, slab_rows)
            sides = []
            for k in range(slab_rows):
                base = base_ref[first + k]
                at = jnp.minimum(base // depth, tiles - 1)
                after = jnp.minimum(at + 1, tiles - 1)
                low = ready[s % 2, :, at].reshape(high, depth)
                top = ready[s % 2, :, after].reshape(high, depth)
                sides.append(jnp.where(lane >= base % depth, low, top).astype(BF16))
            places = place_ref[0, pl.ds(first, slab_rows), :]
            spread_out = [
                jnp.dot(
                    sides[k],
                    jnp.where(slot == places[k : k + 1], 1.0, 0.0).astype(BF16),
                    preferred_element_type=F32,
                )
                for k in range(slab_rows)
            ]
            span = slab_rows * high
            held[pl.ds(pl.multiple_of(first * high, span), span), :] = jnp.concatenate(
                spread_out, axis=0
            )

    @pl.when(step >= spreads)
    def back():
        pair = 2 if coils % 2 == 0 else 1
        mask = mask_ref[0].astype(F32)
        mask = jnp.concatenate([mask, mask], axis=0)
        @pl.loop(0, planes, unroll=math.gcd(planes, UNROLL))
        def one(j):
            x = (step - spreads) * planes + j
            sum_real = sum_imaginary = None
            for c in range(0, coils, pair):
                columns = []
                for k in range(c, c + pair):
                    parts = [
                        held[pl.ds(k * width + 2 * x + p, rows, stride=high), :] for p in range(2)
                    ]
                    columns.append(
                        (lines_ref[k, j].astype(F32) * mask - jnp.concatenate(parts, axis=0)).astype(BF16)
                    )
                turned = jnp.dot(
                    row_ref[...], jnp.concatenate(columns, axis=1), preferred_element_type=F32
                ).astype(BF16)
                stacked = []
                for k in range(pair):
                    part = turned[:, k * depth : (k + 1) * depth]
                    stacked.append(jnp.concatenate([part[:rows], part[rows:]], axis=1))
                images = jnp.dot(
                    jnp.concatenate(stacked, axis=0), depth_ref[...], preferred_element_type=F32
                )
                for k in range(pair):
                    map_real = maps_ref[c + k, j, 0].astype(F32)
                    map_imaginary = maps_ref[c + k, j, 1].astype(F32)
                    back_real = images[k * rows : (k + 1) * rows, :depth]
                    back_imaginary = images[k * rows : (k + 1) * rows, depth:]
                    term_real = map_real * back_real + map_imaginary * back_imaginary
                    term_imaginary = map_real * back_imaginary - map_imaginary * back_real
                    sum_real = term_real if sum_real is None else sum_real + term_real
                    sum_imaginary = (
                        term_imaginary if sum_imaginary is None else sum_imaginary + term_imaginary
                    )
            cosine, sine = phase_ref[j, 0], phase_ref[j, 1]
            out_ref[j, 0] = (cosine * sum_real + sine * sum_imaginary).astype(BF16)
            out_ref[j, 1] = (cosine * sum_imaginary - sine * sum_real).astype(BF16)


def back_images(depth_table, row_table, ranks, data, lines, maps, phase, t, place_in, fit):
    coils, slab, _, rows, depth = maps.shape
    place, mask, base = ranks
    sources = data.shape[0]
    full, shared = fit
    unit, start, planes = place_in
    halved = planes < slab
    width = 2 * planes
    units = (coils * full + (coils // 2) * shared) // (2 if halved else 1)
    block_rows = units * 2 * slab
    step = math.gcd(planes, BACK_PLANES)
    some = math.gcd(sources, SOURCES)
    spreads = sources // some

    def plane(i):
        return jnp.maximum(i - spreads, 0)

    def from_whole(i):
        return start // step + plane(i)

    return pl.pallas_call(
        functools.partial(back_kernel, spreads, fit, halved),
        grid=(spreads + planes // step,),
        in_specs=[
            whole_block(depth_table.shape),
            whole_block(row_table.shape),
            pl.BlockSpec(memory_space=pltpu.SMEM),
            pl.BlockSpec((1, rows, depth), lambda i: (t, 0, 0)),
            pl.BlockSpec((1, rows, depth), lambda i: (t, 0, 0)),
            pl.BlockSpec(
                (some, block_rows, depth),
                lambda i: (jnp.minimum(i, spreads - 1), unit // units, 0),
            ),
            pl.BlockSpec((coils, step, 2 * rows, depth), lambda i: (0, from_whole(i), 0, 0)),
            pl.BlockSpec((coils, step, 2, rows, depth), lambda i: (0, from_whole(i), 0, 0, 0)),
            pl.BlockSpec((step, 2, rows, depth), lambda i: (from_whole(i), 0, 0, 0)),
        ],
        out_specs=pl.BlockSpec((step, 2, rows, depth), lambda i: (plane(i), 0, 0, 0)),
        out_shape=jax.ShapeDtypeStruct((planes, 2, rows, depth), BF16),
        scratch_shapes=[
            pltpu.VMEM((rows * coils * width, depth), F32),
            pltpu.VMEM((2, coils, full + shared, width, depth), F32),
        ],
        compiler_params=params(),
        cost_estimate=cost(3e9, 10e6),
        name="back",
    )(depth_table, row_table, base[t, 0], place, mask, data, lines, maps, phase)


def gradient_kernel(points, halves, block, mix_ref, *rest):
    out_ref = rest[-1]
    ranks, planes, rows2, depth = out_ref.shape
    count = points - 1 + halves
    own_refs, far_refs = rest[:count], rest[count : 2 * count]

    def fill(last):
        chosen = [*range(points - 1), last]
        @pl.loop(0, planes, unroll=math.gcd(planes, UNROLL))
        def one(x):
            for i in range(rows2 // (2 * block)):
                at = slice(i * block, (i + 1) * block)
                columns = [
                    jnp.concatenate([refs[k][x, p, at, :] for k in chosen for p in range(2)], axis=0)
                    for refs in (own_refs, far_refs)
                ]
                both = jnp.dot(
                    mix_ref[...], jnp.concatenate(columns, axis=1), preferred_element_type=F32
                )
                total = both[:, :depth] + both[:, depth:]
                out_ref[:, x, 2 * i * block : 2 * (i + 1) * block, :] = total.reshape(
                    ranks, 2 * block, depth
                )

    if halves == 1:
        fill(points - 1)
    else:
        middle = pl.num_programs(0) // 2
        pl.when(pl.program_id(0) < middle)(lambda: fill(points - 1))
        pl.when(pl.program_id(0) >= middle)(lambda: fill(points))


def gradient(mix, own, far, ranks, points):
    slab, _, rows, depth = own[0].shape
    halves = len(own) - points + 1
    step = math.gcd(slab // halves, GRADIENT_PLANES)
    middle = slab // (2 * step)
    shape = (step, 2, rows, depth)
    blocks = [pl.BlockSpec(shape, lambda x: (x, 0, 0, 0))] * (points if halves == 1 else points - 1)
    if halves == 2:
        blocks.append(pl.BlockSpec(shape, lambda x: (jnp.minimum(x, middle - 1), 0, 0, 0)))
        blocks.append(pl.BlockSpec(shape, lambda x: (jnp.maximum(x - middle, 0), 0, 0, 0)))
    return pl.pallas_call(
        functools.partial(gradient_kernel, points, halves, mix.shape[1] // (2 * points)),
        grid=(slab // step,),
        in_specs=[whole_block(mix.shape)] + blocks * 2,
        out_specs=pl.BlockSpec((ranks, step, 2 * rows, depth), lambda x: (0, x, 0, 0)),
        out_shape=jax.ShapeDtypeStruct((ranks, slab, 2 * rows, depth), F32),
        compiler_params=params(),
        cost_estimate=cost(4e9, 12e6),
        name="gradient",
    )(mix, *own, *far)


def from_other_groups(part, axis):
    groups = lax.axis_size(axis)
    moved = [
        lax.ppermute(part, axis, [(g, (g + shift) % groups) for g in range(groups)])
        for shift in range(1, groups)
    ]
    if groups == 1:
        return jnp.zeros_like(part)
    if groups == 2:
        return moved[0]
    return sum(m.astype(F32) for m in moved).astype(BF16)


def shards(spatial_coef, temporal_basis, coil_maps, field_steps, kspace_data, sample_mask):
    points = temporal_basis.shape[2]
    ranks, slab, rows, _, depth = spatial_coef.shape
    coils = coil_maps.shape[0]
    first, slab_rows = kspace_data.shape[2:4]
    dests = lax.axis_size("space")
    basis = lax.dynamic_slice_in_dim(
        temporal_basis, lax.axis_index("coil") * ranks, ranks, axis=1
    )
    mix, adjoint = mix_factors(basis, 16, False), mix_factors(basis, 32, True)
    data = kspace_data.reshape(coils, points, first, 2 * slab_rows, depth)
    maps = coil_maps.reshape(coils, slab, 2 * rows, depth)
    coef = spatial_coef.reshape(ranks, slab, 2 * rows, depth)
    cells = slab_rows * depth
    half_tiles = -(-SENT_SIXTEENTHS * cells // (8 * depth))
    if coils % 2:
        half_tiles += half_tiles % 2
    fit = (half_tiles // 2, half_tiles % 2)
    slots = half_tiles * depth // 2
    width = 2 * first // dests
    mask_here = sample_mask.astype(BF16)
    held = -(-points * slab_rows // width)
    extra = jnp.pad(
        mask_here.reshape(points * slab_rows, depth),
        ((0, held * width - points * slab_rows), (0, 0)),
    ).reshape(held, width, depth)
    first_table = real_table(first, 1.0, out_interleaved=True)
    depth_forward, depth_back = real_table(depth, -1.0).T, real_table(depth, 1.0).T
    rows_forward, rows_back = real_table(rows, -1.0), real_table(rows, 1.0)

    def prepare(data, start, count, split=False):
        return transform_data(
            first_table, mask_here, extra, data, start, count, dests, fit, split
        )

    def send(sent):
        return lax.all_to_all(sent, "space", split_axis=0, concat_axis=0, tiled=True)

    def back(piece, arrived, lines):
        t, chunk, unit, start, planes_here = piece
        own = back_images(
            depth_back, rows_back, ranked, arrived[chunk], lines[t], planes, phases[t], t,
            (unit, start, planes_here), fit,
        )
        return own, from_other_groups(own, "coil")

    units = coils * fit[0] + (coils // 2) * fit[1]
    head = min(HEAD, points)
    split = points > head and coils % 4 == 0 and slab % 8 == 0
    pieces = [(t, 0, t * units, 0, slab) for t in range(head)]
    pieces += [(t, 1, (t - head) * units, 0, slab) for t in range(head, points)]
    if split:
        last = (points - 1 - head) * units
        pieces[-1] = (points - 1, 1, last, 0, slab // 2)
        pieces.append((points - 1, 2, 0, slab // 2, slab // 2))

    sent = prepare(data, 0, head)
    arrived = [send(sent[0])]
    coef, _ = lax.optimization_barrier((coef, sent[0]))
    turned, phases, planes = make_images(mix, coef, field_steps, maps, points)
    others = [from_other_groups(part, "coil") for part in turned]
    lines = [
        forward_lines(depth_forward, rows_forward, turned[t], others[t], planes)
        for t in range(points)
    ]
    if points > head:
        data, _ = lax.optimization_barrier((data, planes))
        sent = prepare(data, head, points - head, split)
        sent, _ = lax.optimization_barrier((sent, lines[: points - 1]))
        arrived.append(send(sent[0]))
    mask_all = arrived[0][:, head * units * width :].reshape(dests, held * width, depth)
    mask_all = mask_all[:, : points * slab_rows].reshape(dests, points, slab_rows, depth)
    ranked = rank_cells(mask_all, slots)
    early = [back(piece, arrived, lines) for piece in pieces if piece[1] == 0]

    def finish(early, lines, arrived, sent):
        arrived = arrived + [send(part) for part in sent[1:]]
        done = early + [back(piece, arrived, lines) for piece in pieces[len(early) :]]
        own, far = zip(*done)
        return gradient(adjoint, own, far, ranks, points)

    def finish_more(early, lines, arrived, sent):
        count = jnp.cumsum(mask_here.astype(F32).reshape(points, cells), axis=1)
        rest = jnp.where(count > slots, mask_here.reshape(points, cells), 0).astype(BF16)
        rest = rest.reshape(1, points, 1, slab_rows, 1, depth)
        table = real_table(first, 1.0).reshape(2, first, 2, first)
        moved = jnp.einsum(
            "ctxypz,qkpx->ctkqyz", kspace_data * rest, table, preferred_element_type=F32
        ).astype(BF16)
        moved = lax.all_to_all(moved, "space", split_axis=2, concat_axis=4, tiled=True)
        moved = moved.reshape(coils, points, slab, 2 * rows, depth)
        lines = [
            (lines[t].astype(F32) - moved[:, t].astype(F32)).astype(BF16) for t in range(points)
        ]
        early = [back(piece, arrived, lines) for piece in pieces[: len(early)]]
        return finish(early, lines, arrived, sent)

    most = jnp.max(jnp.sum(mask_all.astype(F32), axis=(2, 3)))
    result = lax.cond(most > slots, finish_more, finish, early, lines, arrived, sent)
    return result.reshape(ranks, slab, rows, 2, depth)


def solution(mesh):
    in_specs = (
        P("coil", "space", None, None, None),
        P(),
        P("coil", "space", None, None, None),
        P("space", None, None),
        P("coil", None, None, "space", None, None),
        P(None, "space", None),
    )
    out_specs = P("coil", "space", None, None, None)
    return jax.shard_map(shards, mesh=mesh, in_specs=in_specs, out_specs=out_specs, check_vma=False)
```

profile of v0, /device:TPU:0, one launch (start us, length us, event | category | flops | bytes accessed | tf_op | source)
XLA Modules:
  0.0 169.3 jit_solution(87331551871371576)
XLA Ops:
  0.7 11.2 %data.2 = bf16[16,608,128]{2,1,0:T(8,128)(2,1)} custom-call(bf16[256,256]{1,0:T(8,128)(2,1)} %constant.33.clone.table_ref, bf16[4,8,128]{2,1,0:T(8,128)(2,1)S(1)} %convert_element_type.71.mask_ref, bf16[2,16,128]{2,1,0:T(8,128)(2,1)S(1)} %bitcast.87, bf16[4,4,128,16,128]{4,3,2,1,0:T(8,128)(2,1)} %bitcast.84), custom_call_target="tpu_custom_call" | custom-call | flops 4000000000 | bytes 16000000 | tf_op jit(solution)/shard_map/data/pallas_call | solution.py:311
  12.0 7.7 %all-to-all-start.3 = ((bf16[16,608,128]{2,1,0:T(8,128)(2,1)}), bf16[16,608,128]{2,1,0:T(8,128)(2,1)}, u32[]{:S(2)}, u32[]{:S(2)}) async-start(bf16[16,608,128]{2,1,0:T(8,128)(2,1)} %data.2), calls=%async_computation.3 | async-start | bytes 4980736 | tf_op jit(solution)/shard_map/all_to_all | solution.py:645
  21.0 2.2 %copy-done = bf16[8,8,128,2,128]{4,3,2,1,0:T(2,128)(2,1)S(1)} copy-done((bf16[8,8,128,2,128]{4,3,2,1,0:T(2,128)(2,1)S(1)}, bf16[8,8,128,2,128]{4,3,2,1,0:T(2,128)(2,1)}, u32[]{:S(2)}) %copy-start) | copy-done | bytes 4194328
  23.2 4.8 %images.1 = (bf16[8,2,128,128]{3,2,1,0:T(8,128)(2,1)S(1)}, bf16[8,2,128,128]{3,2,1,0:T(8,128)(2,1)S(1)}, bf16[8,2,128,128]{3,2,1,0:T(8,128)(2,1)S(1)}, bf16[8,2,...) custom-call(bf16[128,256]{1,0:T(8,128)(2,1)S(1)} %copy.34.mix_ref, ...), custom_call_target="tpu_custom_call" | custom-call | flops 4000000000 | bytes 16000000 | tf_op jit(solution)/shard_map/images/pallas_call | solution.py:132
  31.5 11.4 %data.3 = (bf16[16,432,128]{2,1,0:T(8,128)(2,1)}, bf16[16,144,128]{2,1,0:T(8,128)(2,1)}) custom-call(bf16[256,256]{1,0:T(8,128)(2,1)} %constant.33.clone.table_ref, bf16[4,8,128]{2,1,0:T(8,128)(2,1)S(1)} %convert_element_type.71.mask_ref, bf16[2,16,128]{2,1,0:T(8,128)(2,1)S(1)} %bitcast.88, bf16[4,4,128,16,128]{4,3,2,1,0:T(8,128)(2,1)} %bitcast.85), custom_call_target="tpu_custom_call" | custom-call | flops 4000000000 | bytes 16000000 | tf_op jit(solution)/shard_map/data/pallas_call | solution.py:311
  42.9 3.7 %forward.6 = bf16[4,8,256,128]{3,2,1,0:T(8,128)(2,1)} custom-call(bf16[256,256]{1,0:T(8,128)(2,1)S(1)} %copy-done.12, bf16[256,256]{1,0:T(8,128)(2,1)S(1)} %copy-done.17, bf16[8,2,128,128]{3,2,1,0:T(8,128)(2,1)S(1)} %get-tuple-element.151.own_ref, bf16[8,2,128,128]{3,2,1,0:T(8,128)(2,1)S(1)} %collective-permute-done.10.far_ref, ...), custom_call_target="tpu_custom_call" | custom-call | flops 3000000000 | bytes 8000000 | tf_op jit(solution)/shard_map/forward/pallas_call | solution.py:371
  46.6 7.3 %collective-permute-done.9.far_ref = bf16[8,2,128,128]{3,2,1,0:T(8,128)(2,1)S(1)} collective-permute-done((bf16[8,2,128,128]{3,2,1,0:T(8,128)(2,1)S(1)}, bf16[8,2,128,128]{3,2,1,0:T(8,128)(2,1)S(1)}, u32[]{:S(2)}, u32[]{:S(2)}) %collective-permute-start.9) | collective-permute-done | bytes 524320 | tf_op jit(solution)/shard_map/ppermute | solution.py:599
  53.9 2.8 %forward.5.lines_ref = bf16[4,8,256,128]{3,2,1,0:T(8,128)(2,1)S(1)} custom-call(bf16[256,256]{1,0:T(8,128)(2,1)S(1)} %copy-done.12, bf16[256,256]{1,0:T(8,128)(2,1)S(1)} %copy-done.17, bf16[8,2,128,128]{3,2,1,0:T(8,128)(2,1)S(1)} %get-tuple-element.150.own_ref, bf16[8,2,128,128]{3,2,1,0:T(8,128)(2,1)S(1)} %collective-permute-done.9.far_ref, ...), custom_call_target="tpu_custom_call" | custom-call | flops 3000000000 | bytes 8000000 | tf_op jit(solution)/shard_map/forward/pallas_call | solution.py:371
  56.8 7.8 %collective-permute-done.8.far_ref = bf16[8,2,128,128]{3,2,1,0:T(8,128)(2,1)S(1)} collective-permute-done((bf16[8,2,128,128]{3,2,1,0:T(8,128)(2,1)S(1)}, bf16[8,2,128,128]{3,2,1,0:T(8,128)(2,1)S(1)}, u32[]{:S(2)}, u32[]{:S(2)}) %collective-permute-start.8) | collective-permute-done | bytes 524320 | tf_op jit(solution)/shard_map/ppermute | solution.py:599
  64.6 3.7 %forward.4.lines_ref = bf16[4,8,256,128]{3,2,1,0:T(8,128)(2,1)} custom-call(bf16[256,256]{1,0:T(8,128)(2,1)S(1)} %copy-done.12, bf16[256,256]{1,0:T(8,128)(2,1)S(1)} %copy-done.17, bf16[8,2,128,128]{3,2,1,0:T(8,128)(2,1)S(1)} %get-tuple-element.149.own_ref, bf16[8,2,128,128]{3,2,1,0:T(8,128)(2,1)S(1)} %collective-permute-done.8.far_ref, ...), custom_call_target="tpu_custom_call" | custom-call | flops 3000000000 | bytes 8000000 | tf_op jit(solution)/shard_map/forward/pallas_call | solution.py:371
  68.3 12.3 %all-to-all-start.4 = ((bf16[16,432,128]{2,1,0:T(8,128)(2,1)}), bf16[16,432,128]{2,1,0:T(8,128)(2,1)}, u32[]{:S(2)}, u32[]{:S(2)}) async-start(bf16[16,432,128]{2,1,0:T(8,128)(2,1)} %get-tuple-element.152), calls=%async_computation.4 | async-start | bytes 3538944 | tf_op jit(solution)/shard_map/all_to_all | solution.py:645
  83.7 10.1 %back.19 = bf16[8,2,128,128]{3,2,1,0:T(8,128)(2,1)} custom-call(bf16[256,256]{1,0:T(8,128)(2,1)S(1)} %copy-done.17, bf16[256,256]{1,0:T(8,128)(2,1)S(1)} %copy-done.12, s32[128]{0:T(128)S(1)} %get-tuple-element.235.base_ref, f32[4,128,128]{2,1,0:T(8,128)S(1)} %get-tuple-element.142.place_ref, bf16[4,128,128]{2,1,0:T(8,128)(2,1)S(1)} %get-tuple-element.143.mask_ref, ...), custom_call_target="tpu_custom_call" | custom-call | flops 3000000000 | bytes 10000000 | tf_op jit(solution)/shard_map/back/pallas_call | solution.py:513
  94.4 9.1 %back.18 = bf16[8,2,128,128]{3,2,1,0:T(8,128)(2,1)} custom-call(bf16[256,256]{1,0:T(8,128)(2,1)S(1)} %copy-done.17, bf16[256,256]{1,0:T(8,128)(2,1)S(1)} %copy-done.12, s32[128]{0:T(128)S(1)} %get-tuple-element.236.base_ref, f32[4,128,128]{2,1,0:T(8,128)S(1)} %get-tuple-element.142.place_ref, bf16[4,128,128]{2,1,0:T(8,128)(2,1)S(1)} %get-tuple-element.143.mask_ref, ...), custom_call_target="tpu_custom_call" | custom-call | flops 3000000000 | bytes 10000000 | tf_op jit(solution)/shard_map/back/pallas_call | solution.py:513
  106.5 3.9 %forward.7 = bf16[4,8,256,128]{3,2,1,0:T(8,128)(2,1)S(1)} custom-call(bf16[256,256]{1,0:T(8,128)(2,1)S(1)} %copy-done.12, bf16[256,256]{1,0:T(8,128)(2,1)} %constant.34.clone.row_ref.depth_ref, bf16[8,2,128,128]{3,2,1,0:T(8,128)(2,1)S(1)} %get-tuple-element.154.own_ref, bf16[8,2,128,128]{3,2,1,0:T(8,128)(2,1)S(1)} %collective-permute-done.11.far_ref, ...), custom_call_target="tpu_custom_call" | custom-call | flops 3000000000 | bytes 8000000 | tf_op jit(solution)/shard_map/forward/pallas_call | solution.py:371
  112.9 3.1 %all-to-all-done.4 = bf16[16,432,128]{2,1,0:T(8,128)(2,1)} async-done(((bf16[16,432,128]{2,1,0:T(8,128)(2,1)}), bf16[16,432,128]{2,1,0:T(8,128)(2,1)}, u32[]{:S(2)}, u32[]{:S(2)}) %all-to-all-start.4) | async-done | bytes 1769504 | tf_op jit(solution)/shard_map/all_to_all | solution.py:645
  116.0 3.3 %collective-permute-done.12 = bf16[8,2,128,128]{3,2,1,0:T(8,128)(2,1)} collective-permute-done((bf16[8,2,128,128]{3,2,1,0:T(8,128)(2,1)}, bf16[8,2,128,128]{3,2,1,0:T(8,128)(2,1)}, u32[]{:S(2)}, u32[]{:S(2)}) %collective-permute-start.12) | collective-permute-done | bytes 524320 | tf_op jit(solution)/shard_map/ppermute | solution.py:599
  119.3 50.0 %conditional.1 = (f32[8,8,128,2,128]{4,3,2,1,0:T(2,128)}) conditional(s32[]{:T(128)} %convert_element_type.73, (s32[4,8,128]{2,1,0:T(8,128)}, bf16[256,256]{1,0:T(8,128)(2,1)}, bf16[256,256]{1,0:T(8,128)(2,1)S(1)}, f32[4,128,128]{2,1,0:T(8,128)}, bf16[4,128,128]{2,1,0:T(8,128)(2,1)}, /*index=5*/bf16[16,432,128]{2,1,0:T(8,128)(2,1)}, ...), branch_computations={%region_3.4_spmd, %region_4.7_spmd} | conditional | flops 21185765376 | bytes 254025888 | solution.py:707
  119.3 6.6 %all-to-all-start = ((bf16[16,144,128]{2,1,0:T(8,128)(2,1)}), bf16[16,144,128]{2,1,0:T(8,128)(2,1)S(1)}, u32[]{:S(2)}, u32[]{:S(2)}) async-start(bf16[16,144,128]{2,1,0:T(8,128)(2,1)} %get-tuple-element.99), calls=%async_computation | async-start | bytes 1179648 | tf_op jit(solution)/shard_map/cond/branch_0_fun/all_to_all | solution.py:645
  126.7 6.4 %back.11.rest_3_ = bf16[4,2,128,128]{3,2,1,0:T(8,128)(2,1)S(1)} custom-call(bf16[256,256]{1,0:T(8,128)(2,1)} %get-tuple-element.88.depth_ref, bf16[256,256]{1,0:T(8,128)(2,1)S(1)} %get-tuple-element.89.row_ref, s32[128]{0:T(128)S(1)} %get-tuple-element.225.base_ref, f32[4,128,128]{2,1,0:T(8,128)} %get-tuple-element.91.place_ref, ...), custom_call_target="tpu_custom_call" | custom-call | flops 3000000000 | bytes 10000000 | tf_op jit(solution)/shard_map/cond/branch_0_fun/back/pallas_call | solution.py:513
  134.7 8.2 %back.10.rest_2_ = bf16[8,2,128,128]{3,2,1,0:T(8,128)(2,1)S(1)} custom-call(bf16[256,256]{1,0:T(8,128)(2,1)S(1)} %copy-done.18, bf16[256,256]{1,0:T(8,128)(2,1)S(1)} %get-tuple-element.89.row_ref, s32[128]{0:T(128)S(1)} %get-tuple-element.226.base_ref, f32[4,128,128]{2,1,0:T(8,128)S(1)} %copy-done.22, bf16[4,128,128]{2,1,0:T(8,128)(2,1)S(1)} %copy-done.26, ...), custom_call_target="tpu_custom_call" | custom-call | flops 3000000000 | bytes 10000000 | tf_op jit(solution)/shard_map/cond/branch_0_fun/back/pallas_call | solution.py:513
  143.6 6.4 %back.12.rest_4_ = bf16[4,2,128,128]{3,2,1,0:T(8,128)(2,1)S(1)} custom-call(bf16[256,256]{1,0:T(8,128)(2,1)S(1)} %copy-done.19, bf16[256,256]{1,0:T(8,128)(2,1)S(1)} %get-tuple-element.89.row_ref, s32[128]{0:T(128)S(1)} %get-tuple-element.225.base_ref, f32[4,128,128]{2,1,0:T(8,128)S(1)} %copy-done.23, bf16[4,128,128]{2,1,0:T(8,128)(2,1)S(1)} %copy-done.27, ...), custom_call_target="tpu_custom_call" | custom-call | flops 3000000000 | bytes 10000000 | tf_op jit(solution)/shard_map/cond/branch_0_fun/back/pallas_call | solution.py:513
  151.6 6.2 %collective-permute-done.rest_7_ = bf16[8,2,128,128]{3,2,1,0:T(8,128)(2,1)S(1)} collective-permute-done((bf16[8,2,128,128]{3,2,1,0:T(8,128)(2,1)S(1)}, bf16[8,2,128,128]{3,2,1,0:T(8,128)(2,1)S(1)}, u32[]{:S(2)}, u32[]{:S(2)}) %collective-permute-start) | collective-permute-done | bytes 524320 | tf_op jit(solution)/shard_map/cond/branch_0_fun/ppermute | solution.py:599
  157.8 4.8 %collective-permute-done.2.rest_9_ = bf16[4,2,128,128]{3,2,1,0:T(8,128)(2,1)S(1)} collective-permute-done((bf16[4,2,128,128]{3,2,1,0:T(8,128)(2,1)S(1)}, bf16[4,2,128,128]{3,2,1,0:T(8,128)(2,1)S(1)}, u32[]{:S(2)}, u32[]{:S(2)}) %collective-permute-start.2) | collective-permute-done | bytes 262176 | tf_op jit(solution)/shard_map/cond/branch_0_fun/ppermute | solution.py:599
  162.6 6.7 %gradient.2 = f32[8,8,256,128]{3,2,1,0:T(8,128)} custom-call(bf16[512,256]{1,0:T(8,128)(2,1)S(1)} %get-tuple-element.85.mix_ref, bf16[8,2,128,128]{3,2,1,0:T(8,128)(2,1)} %get-tuple-element.86.rest_0_, bf16[8,2,128,128]{3,2,1,0:T(8,128)(2,1)} %get-tuple-element.87.rest_1_, bf16[8,2,128,128]{3,2,1,0:T(8,128)(2,1)S(1)} %back.10.rest_2_, ...), custom_call_target="tpu_custom_call" | custom-call | flops 4000000000 | bytes 12000000 | tf_op jit(solution)/shard_map/cond/branch_0_fun/gradient/pallas_call | solution.py:584
  (88 shorter events, 18.4 us)
Async XLA Ops:
  11.9 9.0 %copy-start.3 = (bf16[256,256]{1,0:T(8,128)(2,1)S(1)}, bf16[256,256]{1,0:T(8,128)(2,1)}, u32[]{:S(2)}) copy-start(bf16[256,256]{1,0:T(8,128)(2,1)} %constant.36.clone.order_ref) | copy-start | bytes 393220
  12.0 56.3 %all-to-all-start.3 = ((bf16[16,608,128]{2,1,0:T(8,128)(2,1)}), bf16[16,608,128]{2,1,0:T(8,128)(2,1)}, u32[]{:S(2)}, u32[]{:S(2)}) async-start(bf16[16,608,128]{2,1,0:T(8,128)(2,1)} %data.2), calls=%async_computation.3 | async-start | bytes 4980736 | tf_op jit(solution)/shard_map/all_to_all | solution.py:645
  28.0 14.9 %collective-permute-start.10 = (bf16[8,2,128,128]{3,2,1,0:T(8,128)(2,1)S(1)}, bf16[8,2,128,128]{3,2,1,0:T(8,128)(2,1)S(1)}, u32[]{:S(2)}, u32[]{:S(2)}) collective-permute-start(bf16[8,2,128,128]{3,2,1,0:T(8,128)(2,1)S(1)} %get-tuple-element.151.own_ref), channel_id=1, source_target_pairs={{0,1},{1,0},{2,3},{3,2},{4,5},{5,4},{6,7},{7,6},{8,9},{9,8},{10,11... | collective-permute-start | bytes 1572872 | tf_op jit(solution)/shard_map/ppermute | solution.py:599
  29.5 24.5 %collective-permute-start.9 = (bf16[8,2,128,128]{3,2,1,0:T(8,128)(2,1)S(1)}, bf16[8,2,128,128]{3,2,1,0:T(8,128)(2,1)S(1)}, u32[]{:S(2)}, u32[]{:S(2)}) collective-permute-start(bf16[8,2,128,128]{3,2,1,0:T(8,128)(2,1)S(1)} %get-tuple-element.150.own_ref), channel_id=1, source_target_pairs={{0,1},{1,0},{2,3},{3,2},{4,5},{5,4},{6,7},{7,6},{8,9},{9,8},{10,11... | collective-permute-start | bytes 1572872 | tf_op jit(solution)/shard_map/ppermute | solution.py:599
  30.0 34.6 %collective-permute-start.8 = (bf16[8,2,128,128]{3,2,1,0:T(8,128)(2,1)S(1)}, bf16[8,2,128,128]{3,2,1,0:T(8,128)(2,1)S(1)}, u32[]{:S(2)}, u32[]{:S(2)}) collective-permute-start(bf16[8,2,128,128]{3,2,1,0:T(8,128)(2,1)S(1)} %get-tuple-element.149.own_ref), channel_id=1, source_target_pairs={{0,1},{1,0},{2,3},{3,2},{4,5},{5,4},{6,7},{7,6},{8,9},{9,8},{10,11... | collective-permute-start | bytes 1572872 | tf_op jit(solution)/shard_map/ppermute | solution.py:599
  31.5 11.4 %copy-start.12 = (bf16[256,256]{1,0:T(8,128)(2,1)S(1)}, bf16[256,256]{1,0:T(8,128)(2,1)}, u32[]{:S(2)}) copy-start(bf16[256,256]{1,0:T(8,128)(2,1)} %constant.35.clone.depth_ref.row_ref) | copy-start | bytes 393220
  31.5 11.4 %copy-start.17 = (bf16[256,256]{1,0:T(8,128)(2,1)S(1)}, bf16[256,256]{1,0:T(8,128)(2,1)}, u32[]{:S(2)}) copy-start(bf16[256,256]{1,0:T(8,128)(2,1)} %constant.34.clone.row_ref.depth_ref) | copy-start | bytes 393220
  31.5 11.4 %copy-start.29 = (bf16[4,8,2,128,128]{4,3,2,1,0:T(8,128)(2,1)S(1)}, bf16[4,8,2,128,128]{4,3,2,1,0:T(8,128)(2,1)}, u32[]{:S(2)}) copy-start(bf16[4,8,2,128,128]{4,3,2,1,0:T(8,128)(2,1)} %get-tuple-element.145.maps_ref) | copy-start | bytes 6291460
  42.9 11.1 %copy-start.30 = (bf16[4,8,2,128,128]{4,3,2,1,0:T(8,128)(2,1)S(1)}, bf16[4,8,2,128,128]{4,3,2,1,0:T(8,128)(2,1)}, u32[]{:S(2)}) copy-start(bf16[4,8,2,128,128]{4,3,2,1,0:T(8,128)(2,1)} %get-tuple-element.145.maps_ref) | copy-start | bytes 6291460
  56.8 26.9 %copy-start.6 = (bf16[4,8,256,128]{3,2,1,0:T(8,128)(2,1)}, bf16[4,8,256,128]{3,2,1,0:T(8,128)(2,1)S(1)}, u32[]{:S(2)}) copy-start(bf16[4,8,256,128]{3,2,1,0:T(8,128)(2,1)S(1)} %forward.5.lines_ref) | copy-start | bytes 6291460
  68.3 47.7 %all-to-all-start.4 = ((bf16[16,432,128]{2,1,0:T(8,128)(2,1)}), bf16[16,432,128]{2,1,0:T(8,128)(2,1)}, u32[]{:S(2)}, u32[]{:S(2)}) async-start(bf16[16,432,128]{2,1,0:T(8,128)(2,1)} %get-tuple-element.152), calls=%async_computation.4 | async-start | bytes 3538944 | tf_op jit(solution)/shard_map/all_to_all | solution.py:645
  80.5 26.0 %collective-permute-start.11 = (bf16[8,2,128,128]{3,2,1,0:T(8,128)(2,1)S(1)}, bf16[8,2,128,128]{3,2,1,0:T(8,128)(2,1)S(1)}, u32[]{:S(2)}, u32[]{:S(2)}) collective-permute-start(bf16[8,2,128,128]{3,2,1,0:T(8,128)(2,1)S(1)} %get-tuple-element.154.own_ref), channel_id=1, source_target_pairs={{0,1},{1,0},{2,3},{3,2},{4,5},{5,4},{6,7},{7,6},{8,9},{9,8},{10,11... | collective-permute-start | bytes 1572872 | tf_op jit(solution)/shard_map/ppermute | solution.py:599
  83.7 10.2 %copy-start.16 = (s32[4,8,128]{2,1,0:T(8,128)}, s32[4,8,128]{2,1,0:T(8,128)S(1)}, u32[]{:S(2)}) copy-start(s32[4,8,128]{2,1,0:T(8,128)S(1)} %get-tuple-element.141) | copy-start | bytes 49156
  83.7 10.7 %copy-start.21 = (f32[4,128,128]{2,1,0:T(8,128)}, f32[4,128,128]{2,1,0:T(8,128)S(1)}, u32[]{:S(2)}) copy-start(f32[4,128,128]{2,1,0:T(8,128)S(1)} %get-tuple-element.142.place_ref) | copy-start | bytes 786436
  83.7 10.7 %copy-start.25 = (bf16[4,128,128]{2,1,0:T(8,128)(2,1)}, bf16[4,128,128]{2,1,0:T(8,128)(2,1)S(1)}, u32[]{:S(2)}) copy-start(bf16[4,128,128]{2,1,0:T(8,128)(2,1)S(1)} %get-tuple-element.143.mask_ref) | copy-start | bytes 393220
  83.7 10.7 %copy-start.7 = (bf16[4,8,256,128]{3,2,1,0:T(8,128)(2,1)S(1)}, bf16[4,8,256,128]{3,2,1,0:T(8,128)(2,1)}, u32[]{:S(2)}) copy-start(bf16[4,8,256,128]{3,2,1,0:T(8,128)(2,1)} %forward.4.lines_ref) | copy-start | bytes 6291460
  83.7 10.7 %copy-start.31 = (bf16[4,8,2,128,128]{4,3,2,1,0:T(8,128)(2,1)S(1)}, bf16[4,8,2,128,128]{4,3,2,1,0:T(8,128)(2,1)}, u32[]{:S(2)}) copy-start(bf16[4,8,2,128,128]{4,3,2,1,0:T(8,128)(2,1)} %get-tuple-element.145.maps_ref) | copy-start | bytes 6291460
  83.7 10.7 %copy-start.34 = (f32[8,2,128,128]{3,2,1,0:T(8,128)S(1)}, f32[8,2,128,128]{3,2,1,0:T(8,128)}, u32[]{:S(2)}) copy-start(f32[8,2,128,128]{3,2,1,0:T(8,128)} %get-tuple-element.157.phase_ref) | copy-start | bytes 3145732
  93.9 22.1 %collective-permute-start.13 = (bf16[8,2,128,128]{3,2,1,0:T(8,128)(2,1)}, bf16[8,2,128,128]{3,2,1,0:T(8,128)(2,1)}, u32[]{:S(2)}, u32[]{:S(2)}) collective-permute-start(bf16[8,2,128,128]{3,2,1,0:T(8,128)(2,1)} %back.19), channel_id=1, source_target_pairs={{0,1},{1,0},{2,3},{3,2},{4,5},{5,4},{6,7},{7,6},{8,9},{9,8},{10,11... | collective-permute-start | bytes 1572872 | tf_op jit(solution)/shard_map/ppermute | solution.py:599
  103.5 15.9 %collective-permute-start.12 = (bf16[8,2,128,128]{3,2,1,0:T(8,128)(2,1)}, bf16[8,2,128,128]{3,2,1,0:T(8,128)(2,1)}, u32[]{:S(2)}, u32[]{:S(2)}) collective-permute-start(bf16[8,2,128,128]{3,2,1,0:T(8,128)(2,1)} %back.18), channel_id=1, source_target_pairs={{0,1},{1,0},{2,3},{3,2},{4,5},{5,4},{6,7},{7,6},{8,9},{9,8},{10,11... | collective-permute-start | bytes 1572872 | tf_op jit(solution)/shard_map/ppermute | solution.py:599
  119.3 24.2 %all-to-all-start = ((bf16[16,144,128]{2,1,0:T(8,128)(2,1)}), bf16[16,144,128]{2,1,0:T(8,128)(2,1)S(1)}, u32[]{:S(2)}, u32[]{:S(2)}) async-start(bf16[16,144,128]{2,1,0:T(8,128)(2,1)} %get-tuple-element.99), calls=%async_computation | async-start | bytes 1179648 | tf_op jit(solution)/shard_map/cond/branch_0_fun/all_to_all | solution.py:645
  133.1 18.5 %collective-permute-start.1 = (bf16[4,2,128,128]{3,2,1,0:T(8,128)(2,1)S(1)}, bf16[4,2,128,128]{3,2,1,0:T(8,128)(2,1)S(1)}, u32[]{:S(2)}, u32[]{:S(2)}) collective-permute-start(bf16[4,2,128,128]{3,2,1,0:T(8,128)(2,1)S(1)} %back.11.rest_3_), channel_id=1, source_target_pairs={{0,1},{1,0},{2,3},{3,2},{4,5},{5,4},{6,7},{7,6},{8,9},{9,8},{10,11... | collective-permute-start | bytes 786440 | tf_op jit(solution)/shard_map/cond/branch_0_fun/ppermute | solution.py:599
  143.0 14.8 %collective-permute-start = (bf16[8,2,128,128]{3,2,1,0:T(8,128)(2,1)S(1)}, bf16[8,2,128,128]{3,2,1,0:T(8,128)(2,1)S(1)}, u32[]{:S(2)}, u32[]{:S(2)}) collective-permute-start(bf16[8,2,128,128]{3,2,1,0:T(8,128)(2,1)S(1)} %back.10.rest_2_), channel_id=1, source_target_pairs={{0,1},{1,0},{2,3},{3,2},{4,5},{5,4},{6,7},{7,6},{8,9},{9,8},{10,11... | collective-permute-start | bytes 1572872 | tf_op jit(solution)/shard_map/cond/branch_0_fun/ppermute | solution.py:599
  150.0 12.6 %collective-permute-start.2 = (bf16[4,2,128,128]{3,2,1,0:T(8,128)(2,1)S(1)}, bf16[4,2,128,128]{3,2,1,0:T(8,128)(2,1)S(1)}, u32[]{:S(2)}, u32[]{:S(2)}) collective-permute-start(bf16[4,2,128,128]{3,2,1,0:T(8,128)(2,1)S(1)} %back.12.rest_4_), channel_id=1, source_target_pairs={{0,1},{1,0},{2,3},{3,2},{4,5},{5,4},{6,7},{7,6},{8,9},{9,8},{10,11... | collective-permute-start | bytes 786440 | tf_op jit(solution)/shard_map/cond/branch_0_fun/ppermute | solution.py:599
  (14 other events, 110.1 us)
where the time goes:
time: 170 us; the launch traced here: 169 us
  Pallas kernels  88.9 us (52%)
  starting transfers between devices  37.4 us (22%)
  waiting for transfers between devices  32.7 us (19%)
  local copies, waits for them, and re-layouts  5.49 us (3%)
  other arithmetic  3.77 us (2%)
    pallas_call x5, Pallas kernels, back_images(): pl.pallas_call(functools.partial(back_kernel, spreads, fit, halved), grid...  40.2 us
    ppermute x9, waiting for transfers between devices, from_other_groups(): lax.ppermute(part, axis, [(g, (g + shift) % groups) for g in range(groups)])  29.5 us
    all_to_all x3, starting transfers between devices, send(): lax.all_to_all(sent, 'space', split_axis=0, concat_axis=0, tiled=True)  26.6 us
    pallas_call x2, Pallas kernels, transform_data(): pl.pallas_call(functools.partial(data_kernel, full, shared, split, more),...  22.6 us
    pallas_call x4, Pallas kernels, forward_lines(): pl.pallas_call(forward_kernel, grid=(slab // step,), in_specs=[whole_bloc...  14.1 us
    ppermute x9, starting transfers between devices, from_other_groups(): lax.ppermute(part, axis, [(g, (g + shift) % groups) for g in range(groups)])  10.9 us
    pallas_call x1, Pallas kernels, gradient(): pl.pallas_call(functools.partial(gradient_kernel, points, halves, mix.sha...  6.69 us
    pallas_call x1, Pallas kernels, make_images(): pl.pallas_call(functools.partial(image_kernel, points, mix.shape[0] // (2...  4.81 us
  transfers between devices with their start and end apart: 12, of which 6 were waited for; matrix products, arithmetic and copies ran while one was open for 4% of the time, Pallas kernels for 42%

commit v1 on v0

--- a/solution.py
+++ b/solution.py
@@ -16,7 +16,9 @@
 BACK_PLANES = 8
 SOURCES = 8
 HEAD = 2
-UNROLL = 2
+IMAGE_UNROLL = 1
+FORWARD_UNROLL = 2
+BACK_UNROLL = 2
 GRADIENT_PLANES = 2
 VMEM_BYTES = 24 * 2**20
 F32 = jnp.float32
@@ -79,7 +81,7 @@
     coils = maps_ref.shape[0]
     rows = rows2 // 2
     blocks = rows // block
-    @pl.loop(0, planes, unroll=math.gcd(planes, UNROLL))
+    @pl.loop(0, planes, unroll=math.gcd(planes, IMAGE_UNROLL))
     def one(x):
         pair = 2 if blocks % 2 == 0 else 1
         for i in range(0, blocks, pair):
@@ -332,7 +334,7 @@
 def forward_kernel(depth_ref, row_ref, own_ref, far_ref, maps_ref, out_ref):
     coils, planes, _, rows, depth = maps_ref.shape
     pair = 2 if coils % 2 == 0 else 1
-    @pl.loop(0, planes, unroll=math.gcd(planes, UNROLL))
+    @pl.loop(0, planes, unroll=math.gcd(planes, FORWARD_UNROLL))
     def one(x):
         real = own_ref[x, 0].astype(F32) + far_ref[x, 0].astype(F32)
         imaginary = own_ref[x, 1].astype(F32) + far_ref[x, 1].astype(F32)
@@ -409,7 +411,7 @@
     def spread():
         lane = lax.broadcasted_iota(jnp.int32, (high, depth), 1)
         slot = lax.broadcasted_iota(jnp.int32, (depth, depth), 0).astype(F32)
-        @pl.loop(0, sources, unroll=math.gcd(sources, UNROLL))
+        @pl.loop(0, sources, unroll=math.gcd(sources, BACK_UNROLL))
         def one(s):
             for c in range(coils):
                 for i in range(full):
@@ -451,7 +453,7 @@
         pair = 2 if coils % 2 == 0 else 1
         mask = mask_ref[0].astype(F32)
         mask = jnp.concatenate([mask, mask], axis=0)
-        @pl.loop(0, planes, unroll=math.gcd(planes, UNROLL))
+        @pl.loop(0, planes, unroll=math.gcd(planes, BACK_UNROLL))
         def one(j):
             x = (step - spreads) * planes + j
             sum_real = sum_imaginary = None
@@ -539,58 +541,54 @@
     )(depth_table, row_table, base[t, 0], place, mask, data, lines, maps, phase)
 
 
-def gradient_kernel(points, halves, block, mix_ref, *rest):
-    out_ref = rest[-1]
+def gradient_kernel(points, block, mix_ref, *rest):
+    own_refs, far_refs, out_ref = rest[:points], rest[points : 2 * points], rest[-1]
     ranks, planes, rows2, depth = out_ref.shape
-    count = points - 1 + halves
-    own_refs, far_refs = rest[:count], rest[count : 2 * count]
-
-    def fill(last):
-        chosen = [*range(points - 1), last]
-        @pl.loop(0, planes, unroll=math.gcd(planes, UNROLL))
-        def one(x):
-            for i in range(rows2 // (2 * block)):
-                at = slice(i * block, (i + 1) * block)
-                columns = [
-                    jnp.concatenate([refs[k][x, p, at, :] for k in chosen for p in range(2)], axis=0)
-                    for refs in (own_refs, far_refs)
-                ]
-                both = jnp.dot(
-                    mix_ref[...], jnp.concatenate(columns, axis=1), preferred_element_type=F32
+    @pl.loop(0, planes, unroll=math.gcd(planes, BACK_UNROLL))
+    def one(x):
+        for i in range(rows2 // (2 * block)):
+            at = slice(i * block, (i + 1) * block)
+            columns = [
+                jnp.concatenate(
+                    [refs[t][x, p, at, :] for t in range(points) for p in range(2)], axis=0
                 )
-                total = both[:, :depth] + both[:, depth:]
-                out_ref[:, x, 2 * i * block : 2 * (i + 1) * block, :] = total.reshape(
-                    ranks, 2 * block, depth
-                )
-
-    if halves == 1:
-        fill(points - 1)
-    else:
-        middle = pl.num_programs(0) // 2
-        pl.when(pl.program_id(0) < middle)(lambda: fill(points - 1))
-        pl.when(pl.program_id(0) >= middle)(lambda: fill(points))
-
-
-def gradient(mix, own, far, ranks, points):
-    slab, _, rows, depth = own[0].shape
-    halves = len(own) - points + 1
-    step = math.gcd(slab // halves, GRADIENT_PLANES)
-    middle = slab // (2 * step)
-    shape = (step, 2, rows, depth)
-    blocks = [pl.BlockSpec(shape, lambda x: (x, 0, 0, 0))] * (points if halves == 1 else points - 1)
-    if halves == 2:
-        blocks.append(pl.BlockSpec(shape, lambda x: (jnp.minimum(x, middle - 1), 0, 0, 0)))
-        blocks.append(pl.BlockSpec(shape, lambda x: (jnp.maximum(x - middle, 0), 0, 0, 0)))
+                for refs in (own_refs, far_refs)
+            ]
+            both = jnp.dot(
+                mix_ref[...], jnp.concatenate(columns, axis=1), preferred_element_type=F32
+            )
+            total = both[:, :depth] + both[:, depth:]
+            out_ref[:, x, 2 * i * block : 2 * (i + 1) * block, :] = total.reshape(
+                ranks, 2 * block, depth
+            )
+
+
+def gradient(mix, own, far, ranks, slab, start, planes, before):
+    points = len(own)
+    _, _, rows, depth = own[0].shape
+    step = math.gcd(planes, GRADIENT_PLANES)
+
+    def block(part):
+        first = start // step if part.shape[0] == slab else 0
+        return pl.BlockSpec((step, 2, rows, depth), lambda x: (first + x, 0, 0, 0))
+
+    parts = [*own, *far]
+    more = [] if before is None else [before]
     return pl.pallas_call(
-        functools.partial(gradient_kernel, points, halves, mix.shape[1] // (2 * points)),
-        grid=(slab // step,),
-        in_specs=[whole_block(mix.shape)] + blocks * 2,
-        out_specs=pl.BlockSpec((ranks, step, 2 * rows, depth), lambda x: (0, x, 0, 0)),
+        functools.partial(gradient_kernel, points, mix.shape[1] // (2 * points)),
+        grid=(planes // step,),
+        in_specs=[whole_block(mix.shape)]
+        + [block(part) for part in parts]
+        + [pl.BlockSpec(memory_space=pl.ANY)] * len(more),
+        out_specs=pl.BlockSpec(
+            (ranks, step, 2 * rows, depth), lambda x: (0, start // step + x, 0, 0)
+        ),
         out_shape=jax.ShapeDtypeStruct((ranks, slab, 2 * rows, depth), F32),
+        input_output_aliases={1 + len(parts): 0} if more else {},
         compiler_params=params(),
         cost_estimate=cost(4e9, 12e6),
         name="gradient",
-    )(mix, *own, *far)
+    )(mix, *parts, *more)
 
 
 def from_other_groups(part, axis):
@@ -683,9 +681,20 @@
 
     def finish(early, lines, arrived, sent):
         arrived = arrived + [send(part) for part in sent[1:]]
-        done = early + [back(piece, arrived, lines) for piece in pieces[len(early) :]]
+        done = list(early)
+        for piece in pieces[len(early) :]:
+            behind = list(lines)
+            behind[piece[0]], _ = lax.optimization_barrier((lines[piece[0]], done[-1][0]))
+            done.append(back(piece, arrived, behind))
         own, far = zip(*done)
-        return gradient(adjoint, own, far, ranks, points)
+        out = None
+        for i in range(points - 1, len(pieces)):
+            whole = [*range(points - 1), i]
+            out = gradient(
+                adjoint, [own[k] for k in whole], [far[k] for k in whole], ranks, slab,
+                *pieces[i][3:], out,
+            )
+        return out
 
     def finish_more(early, lines, arrived, sent):
         count = jnp.cumsum(mask_here.astype(F32).reshape(points, cells), axis=1)

time: 170 us -> 166 us (0.976)
  starting transfers between devices: 37.4 us -> 33.4 us
  Pallas kernels: 88.9 us -> 92.6 us
  waiting for transfers between devices: 32.7 us -> 29.7 us
    all_to_all x3, starting transfers between devices: 26.6 us -> 22.5 us  [send(): lax.all_to_all(sent, 'space', split_axis=0, concat_axis=0, tiled=True)]
    ppermute x9, waiting for transfers between devices: 29.5 us -> 26.9 us  [from_other_groups(): lax.ppermute(part, axis, [(g, (g + shift) % groups) for g in range(groups)])]
    pallas_call x4, Pallas kernels: 14.1 us -> 16.4 us  [forward_lines(): pl.pallas_call(forward_kernel, grid=(slab // step,), in_specs=[whole_bloc...]
    pallas_call x1 -> x2, Pallas kernels: 6.69 us -> 7.51 us  [gradient(): pl.pallas_call(functools.partial(gradient_kernel, points, mix.shape[1] //...]
  transfers between devices with their start and end apart: 12 -> 12, of which waited for: 6 -> 5; matrix products, arithmetic and copies ran while one was open for 4% -> 3% of each run, Pallas kernels for 42% -> 47%
where the time goes in v1:
time: 166 us; the launch traced here: 165 us
  Pallas kernels  92.6 us (56%)
  starting transfers between devices  33.4 us (20%)
  waiting for transfers between devices  29.7 us (18%)
  local copies, waits for them, and re-layouts  4.81 us (3%)
  other arithmetic  3.76 us (2%)
    pallas_call x5, Pallas kernels, back_images(): pl.pallas_call(functools.partial(back_kernel, spreads, fit, halved), grid...  40.5 us
    ppermute x9, waiting for transfers between devices, from_other_groups(): lax.ppermute(part, axis, [(g, (g + shift) % groups) for g in range(groups)])  26.9 us
    pallas_call x2, Pallas kernels, transform_data(): pl.pallas_call(functools.partial(data_kernel, full, shared, split, more),...  22.5 us
    all_to_all x3, starting transfers between devices, send(): lax.all_to_all(sent, 'space', split_axis=0, concat_axis=0, tiled=True)  22.5 us
    pallas_call x4, Pallas kernels, forward_lines(): pl.pallas_call(forward_kernel, grid=(slab // step,), in_specs=[whole_bloc...  16.4 us
    ppermute x9, starting transfers between devices, from_other_groups(): lax.ppermute(part, axis, [(g, (g + shift) % groups) for g in range(groups)])  10.9 us
    pallas_call x2, Pallas kernels, gradient(): pl.pallas_call(functools.partial(gradient_kernel, points, mix.shape[1] //...  7.51 us
    pallas_call x1, Pallas kernels, make_images(): pl.pallas_call(functools.partial(image_kernel, points, mix.shape[0] // (2...  5.24 us
  transfers between devices with their start and end apart: 12, of which 5 were waited for; matrix products, arithmetic and copies ran while one was open for 3% of the time, Pallas kernels for 47%

profile of v1, /device:TPU:0, one launch (start us, length us, event | category | flops | bytes accessed | tf_op | source)
XLA Modules:
  0.0 165.3 jit_solution(10344090244276578435)
XLA Ops:
  0.7 11.2 %data.2 = bf16[16,608,128]{2,1,0:T(8,128)(2,1)} custom-call(bf16[256,256]{1,0:T(8,128)(2,1)} %constant.33.clone.table_ref, bf16[4,8,128]{2,1,0:T(8,128)(2,1)S(1)} %convert_element_type.71.mask_ref, bf16[2,16,128]{2,1,0:T(8,128)(2,1)S(1)} %bitcast.87, bf16[4,4,128,16,128]{4,3,2,1,0:T(8,128)(2,1)} %bitcast.84), custom_call_target="tpu_custom_call" | custom-call | flops 4000000000 | bytes 16000000 | tf_op jit(solution)/shard_map/data/pallas_call | solution.py:313
  12.0 7.7 %all-to-all-start.3 = ((bf16[16,608,128]{2,1,0:T(8,128)(2,1)}), bf16[16,608,128]{2,1,0:T(8,128)(2,1)}, u32[]{:S(2)}, u32[]{:S(2)}) async-start(bf16[16,608,128]{2,1,0:T(8,128)(2,1)} %data.2), calls=%async_computation.3 | async-start | bytes 4980736 | tf_op jit(solution)/shard_map/all_to_all | solution.py:643
  21.0 2.2 %copy-done = bf16[8,8,128,2,128]{4,3,2,1,0:T(2,128)(2,1)S(1)} copy-done((bf16[8,8,128,2,128]{4,3,2,1,0:T(2,128)(2,1)S(1)}, bf16[8,8,128,2,128]{4,3,2,1,0:T(2,128)(2,1)}, u32[]{:S(2)}) %copy-start) | copy-done | bytes 4194328
  23.2 5.2 %images.1 = (bf16[8,2,128,128]{3,2,1,0:T(8,128)(2,1)S(1)}, bf16[8,2,128,128]{3,2,1,0:T(8,128)(2,1)S(1)}, bf16[8,2,128,128]{3,2,1,0:T(8,128)(2,1)S(1)}, bf16[8,2,...) custom-call(bf16[128,256]{1,0:T(8,128)(2,1)S(1)} %copy.36.mix_ref, ...), custom_call_target="tpu_custom_call" | custom-call | flops 4000000000 | bytes 16000000 | tf_op jit(solution)/shard_map/images/pallas_call | solution.py:134
  31.9 11.3 %data.3 = (bf16[16,432,128]{2,1,0:T(8,128)(2,1)}, bf16[16,144,128]{2,1,0:T(8,128)(2,1)}) custom-call(bf16[256,256]{1,0:T(8,128)(2,1)} %constant.33.clone.table_ref, bf16[4,8,128]{2,1,0:T(8,128)(2,1)S(1)} %convert_element_type.71.mask_ref, bf16[2,16,128]{2,1,0:T(8,128)(2,1)S(1)} %bitcast.88, bf16[4,4,128,16,128]{4,3,2,1,0:T(8,128)(2,1)} %bitcast.85), custom_call_target="tpu_custom_call" | custom-call | flops 4000000000 | bytes 16000000 | tf_op jit(solution)/shard_map/data/pallas_call | solution.py:313
  43.2 4.1 %forward.6.lines_ref = bf16[4,8,256,128]{3,2,1,0:T(8,128)(2,1)S(1)} custom-call(bf16[256,256]{1,0:T(8,128)(2,1)S(1)} %copy-done.10, bf16[256,256]{1,0:T(8,128)(2,1)S(1)} %copy-done.17, bf16[8,2,128,128]{3,2,1,0:T(8,128)(2,1)S(1)} %get-tuple-element.158.own_ref, bf16[8,2,128,128]{3,2,1,0:T(8,128)(2,1)S(1)} %collective-permute-done.10.far_ref, ...), custom_call_target="tpu_custom_call" | custom-call | flops 3000000000 | bytes 8000000 | tf_op jit(solution)/shard_map/forward/pallas_call | solution.py:373
  47.3 17.7 %collective-permute-done.9.far_ref = bf16[8,2,128,128]{3,2,1,0:T(8,128)(2,1)S(1)} collective-permute-done((bf16[8,2,128,128]{3,2,1,0:T(8,128)(2,1)S(1)}, bf16[8,2,128,128]{3,2,1,0:T(8,128)(2,1)S(1)}, u32[]{:S(2)}, u32[]{:S(2)}) %collective-permute-start.9) | collective-permute-done | bytes 524320 | tf_op jit(solution)/shard_map/ppermute | solution.py:597
  65.0 3.7 %forward.5.lines_ref = bf16[4,8,256,128]{3,2,1,0:T(8,128)(2,1)} custom-call(bf16[256,256]{1,0:T(8,128)(2,1)S(1)} %copy-done.10, bf16[256,256]{1,0:T(8,128)(2,1)S(1)} %copy-done.17, bf16[8,2,128,128]{3,2,1,0:T(8,128)(2,1)S(1)} %get-tuple-element.153.own_ref, bf16[8,2,128,128]{3,2,1,0:T(8,128)(2,1)S(1)} %collective-permute-done.9.far_ref, ...), custom_call_target="tpu_custom_call" | custom-call | flops 3000000000 | bytes 8000000 | tf_op jit(solution)/shard_map/forward/pallas_call | solution.py:373
  68.7 3.7 %forward.4 = bf16[4,8,256,128]{3,2,1,0:T(8,128)(2,1)} custom-call(bf16[256,256]{1,0:T(8,128)(2,1)S(1)} %copy-done.10, bf16[256,256]{1,0:T(8,128)(2,1)S(1)} %copy-done.17, bf16[8,2,128,128]{3,2,1,0:T(8,128)(2,1)S(1)} %get-tuple-element.149.own_ref, bf16[8,2,128,128]{3,2,1,0:T(8,128)(2,1)S(1)} %collective-permute-done.8.far_ref, ...), custom_call_target="tpu_custom_call" | custom-call | flops 3000000000 | bytes 8000000 | tf_op jit(solution)/shard_map/forward/pallas_call | solution.py:373
  72.4 8.1 %all-to-all-start.4 = ((bf16[16,432,128]{2,1,0:T(8,128)(2,1)}), bf16[16,432,128]{2,1,0:T(8,128)(2,1)}, u32[]{:S(2)}, u32[]{:S(2)}) async-start(bf16[16,432,128]{2,1,0:T(8,128)(2,1)} %get-tuple-element.159), calls=%async_computation.4 | async-start | bytes 3538944 | tf_op jit(solution)/shard_map/all_to_all | solution.py:643
  80.5 1.6 collective-permute-start.11
  83.8 10.1 %back.19 = bf16[8,2,128,128]{3,2,1,0:T(8,128)(2,1)} custom-call(bf16[256,256]{1,0:T(8,128)(2,1)S(1)} %copy-done.17, bf16[256,256]{1,0:T(8,128)(2,1)S(1)} %copy-done.10, s32[128]{0:T(128)S(1)} %get-tuple-element.241.base_ref, f32[4,128,128]{2,1,0:T(8,128)S(1)} %get-tuple-element.151.place_ref, bf16[4,128,128]{2,1,0:T(8,128)(2,1)S(1)} %get-tuple-element.152.mask_ref, ...), custom_call_target="tpu_custom_call" | custom-call | flops 3000000000 | bytes 10000000 | tf_op jit(solution)/shard_map/back/pallas_call | solution.py:515
  94.4 8.3 %back.18 = bf16[8,2,128,128]{3,2,1,0:T(8,128)(2,1)S(1)} custom-call(bf16[256,256]{1,0:T(8,128)(2,1)S(1)} %copy-done.18, bf16[256,256]{1,0:T(8,128)(2,1)S(1)} %copy-done.11, s32[128]{0:T(128)S(1)} %get-tuple-element.242.base_ref, f32[4,128,128]{2,1,0:T(8,128)S(1)} %get-tuple-element.151.place_ref, bf16[4,128,128]{2,1,0:T(8,128)(2,1)S(1)} %get-tuple-element.152.mask_ref, ...), custom_call_target="tpu_custom_call" | custom-call | flops 3000000000 | bytes 10000000 | tf_op jit(solution)/shard_map/back/pallas_call | solution.py:515
  105.8 5.0 %forward.7 = bf16[4,8,256,128]{3,2,1,0:T(8,128)(2,1)} custom-call(bf16[256,256]{1,0:T(8,128)(2,1)} %constant.35.clone.depth_ref.row_ref, bf16[256,256]{1,0:T(8,128)(2,1)} %constant.34.clone.row_ref.depth_ref, bf16[8,2,128,128]{3,2,1,0:T(8,128)(2,1)S(1)} %get-tuple-element.162.own_ref, bf16[8,2,128,128]{3,2,1,0:T(8,128)(2,1)S(1)} %collective-permute-done.11.far_ref, ...), custom_call_target="tpu_custom_call" | custom-call | flops 3000000000 | bytes 8000000 | tf_op jit(solution)/shard_map/forward/pallas_call | solution.py:373
  113.2 2.8 %all-to-all-done.4 = bf16[16,432,128]{2,1,0:T(8,128)(2,1)} async-done(((bf16[16,432,128]{2,1,0:T(8,128)(2,1)}), bf16[16,432,128]{2,1,0:T(8,128)(2,1)}, u32[]{:S(2)}, u32[]{:S(2)}) %all-to-all-start.4) | async-done | bytes 1769504 | tf_op jit(solution)/shard_map/all_to_all | solution.py:643
  116.0 3.3 %collective-permute-done.13 = bf16[8,2,128,128]{3,2,1,0:T(8,128)(2,1)} collective-permute-done((bf16[8,2,128,128]{3,2,1,0:T(8,128)(2,1)S(1)}, bf16[8,2,128,128]{3,2,1,0:T(8,128)(2,1)}, u32[]{:S(2)}, u32[]{:S(2)}) %collective-permute-start.13) | collective-permute-done | bytes 524320 | tf_op jit(solution)/shard_map/ppermute | solution.py:597
  119.3 46.0 %conditional.1 = (f32[8,8,128,2,128]{4,3,2,1,0:T(2,128)}) conditional(s32[]{:T(128)} %convert_element_type.73, (s32[4,8,128]{2,1,0:T(8,128)S(1)}, bf16[4,8,256,128]{3,2,1,0:T(8,128)(2,1)}, bf16[8,2,128,128]{3,2,1,0:T(8,128)(2,1)S(1)}, bf16[256,256]{1,0:T(8,128)(2,1)}, bf16[256,256]{1,0:T(8,128)(2,1)S(1)}, /*index=5*/f32[4,128,128]{2,1,0:T(8,128)}, ...), branch_computations={%region_3.4_spmd, %region_4.7_spmd} | conditional | flops 25185765376 | bytes 257637248 | solution.py:716
  119.3 6.6 %all-to-all-start = ((bf16[16,144,128]{2,1,0:T(8,128)(2,1)}), bf16[16,144,128]{2,1,0:T(8,128)(2,1)S(1)}, u32[]{:S(2)}, u32[]{:S(2)}) async-start(bf16[16,144,128]{2,1,0:T(8,128)(2,1)} %get-tuple-element.98), calls=%async_computation | async-start | bytes 1179648 | tf_op jit(solution)/shard_map/cond/branch_0_fun/all_to_all | solution.py:643
  126.0 10.0 %back.10.rest_2_ = bf16[8,2,128,128]{3,2,1,0:T(8,128)(2,1)S(1)} custom-call(bf16[256,256]{1,0:T(8,128)(2,1)} %get-tuple-element.88.depth_ref, bf16[256,256]{1,0:T(8,128)(2,1)S(1)} %get-tuple-element.89.row_ref, s32[128]{0:T(128)S(1)} %get-tuple-element.232.base_ref, f32[4,128,128]{2,1,0:T(8,128)} %get-tuple-element.91.place_ref, ...), custom_call_target="tpu_custom_call" | custom-call | flops 3000000000 | bytes 10000000 | tf_op jit(solution)/shard_map/cond/branch_0_fun/back/pallas_call | solution.py:515
  137.6 5.7 %back.11.rest_3_ = bf16[4,2,128,128]{3,2,1,0:T(8,128)(2,1)S(1)} custom-call(bf16[256,256]{1,0:T(8,128)(2,1)S(1)} %copy-done.19, bf16[256,256]{1,0:T(8,128)(2,1)S(1)} %get-tuple-element.89.row_ref, s32[128]{0:T(128)S(1)} %get-tuple-element.231.base_ref, f32[4,128,128]{2,1,0:T(8,128)S(1)} %copy-done.22, bf16[4,128,128]{2,1,0:T(8,128)(2,1)S(1)} %copy-done.25, ...), custom_call_target="tpu_custom_call" | custom-call | flops 3000000000 | bytes 10000000 | tf_op jit(solution)/shard_map/cond/branch_0_fun/back/pallas_call | solution.py:515
  143.9 6.5 %back.12.rest_3_ = bf16[4,2,128,128]{3,2,1,0:T(8,128)(2,1)S(1)} custom-call(bf16[256,256]{1,0:T(8,128)(2,1)} %get-tuple-element.88.depth_ref, bf16[256,256]{1,0:T(8,128)(2,1)} %copy-done.13, s32[128]{0:T(128)S(1)} %get-tuple-element.231.base_ref, f32[4,128,128]{2,1,0:T(8,128)} %get-tuple-element.91.place_ref, ...), custom_call_target="tpu_custom_call" | custom-call | flops 3000000000 | bytes 10000000 | tf_op jit(solution)/shard_map/cond/branch_0_fun/back/pallas_call | solution.py:515
  152.0 4.4 %collective-permute-done.2.rest_7_ = bf16[4,2,128,128]{3,2,1,0:T(8,128)(2,1)S(1)} collective-permute-done((bf16[4,2,128,128]{3,2,1,0:T(8,128)(2,1)S(1)}, bf16[4,2,128,128]{3,2,1,0:T(8,128)(2,1)S(1)}, u32[]{:S(2)}, u32[]{:S(2)}) %collective-permute-start.2) | collective-permute-done | bytes 262176 | tf_op jit(solution)/shard_map/cond/branch_0_fun/ppermute | solution.py:597
  156.4 3.8 %gradient.4.rest_8_ = f32[8,8,256,128]{3,2,1,0:T(8,128)} custom-call(bf16[512,256]{1,0:T(8,128)(2,1)S(1)} %get-tuple-element.85.mix_ref, bf16[8,2,128,128]{3,2,1,0:T(8,128)(2,1)} %get-tuple-element.86.rest_0_, bf16[8,2,128,128]{3,2,1,0:T(8,128)(2,1)S(1)} %get-tuple-element.87.rest_1_, bf16[8,2,128,128]{3,2,1,0:T(8,128)(2,1)S(1)} %back.10.rest_2_, ...), custom_call_target="tpu_custom_call" | custom-call | flops 4000000000 | bytes 12000000 | tf_op jit(solution)/shard_map/cond/branch_0_fun/gradient/pallas_call | solution.py:577
  161.6 3.8 %gradient.5 = f32[8,8,256,128]{3,2,1,0:T(8,128)} custom-call(bf16[512,256]{1,0:T(8,128)(2,1)S(1)} %get-tuple-element.85.mix_ref, bf16[8,2,128,128]{3,2,1,0:T(8,128)(2,1)} %get-tuple-element.86.rest_0_, bf16[8,2,128,128]{3,2,1,0:T(8,128)(2,1)S(1)} %get-tuple-element.87.rest_1_, ...), custom_call_target="tpu_custom_call", output_to_operand_aliasing={{}: (9, {})} | custom-call | flops 4000000000 | bytes 12000000 | tf_op jit(solution)/shard_map/cond/branch_0_fun/gradient/pallas_call | solution.py:577
  (85 shorter events, 17.6 us)
Async XLA Ops:
  12.0 60.5 %all-to-all-start.3 = ((bf16[16,608,128]{2,1,0:T(8,128)(2,1)}), bf16[16,608,128]{2,1,0:T(8,128)(2,1)}, u32[]{:S(2)}, u32[]{:S(2)}) async-start(bf16[16,608,128]{2,1,0:T(8,128)(2,1)} %data.2), calls=%async_computation.3 | async-start | bytes 4980736 | tf_op jit(solution)/shard_map/all_to_all | solution.py:643
  28.4 14.8 %collective-permute-start.10 = (bf16[8,2,128,128]{3,2,1,0:T(8,128)(2,1)S(1)}, bf16[8,2,128,128]{3,2,1,0:T(8,128)(2,1)S(1)}, u32[]{:S(2)}, u32[]{:S(2)}) collective-permute-start(bf16[8,2,128,128]{3,2,1,0:T(8,128)(2,1)S(1)} %get-tuple-element.158.own_ref), channel_id=1, source_target_pairs={{0,1},{1,0},{2,3},{3,2},{4,5},{5,4},{6,7},{7,6},{8,9},{9,8},{10,11... | collective-permute-start | bytes 1572872 | tf_op jit(solution)/shard_map/ppermute | solution.py:597
  29.9 38.8 %collective-permute-start.8 = (bf16[8,2,128,128]{3,2,1,0:T(8,128)(2,1)S(1)}, bf16[8,2,128,128]{3,2,1,0:T(8,128)(2,1)S(1)}, u32[]{:S(2)}, u32[]{:S(2)}) collective-permute-start(bf16[8,2,128,128]{3,2,1,0:T(8,128)(2,1)S(1)} %get-tuple-element.149.own_ref), channel_id=1, source_target_pairs={{0,1},{1,0},{2,3},{3,2},{4,5},{5,4},{6,7},{7,6},{8,9},{9,8},{10,11... | collective-permute-start | bytes 1572872 | tf_op jit(solution)/shard_map/ppermute | solution.py:597
  30.4 34.6 %collective-permute-start.9 = (bf16[8,2,128,128]{3,2,1,0:T(8,128)(2,1)S(1)}, bf16[8,2,128,128]{3,2,1,0:T(8,128)(2,1)S(1)}, u32[]{:S(2)}, u32[]{:S(2)}) collective-permute-start(bf16[8,2,128,128]{3,2,1,0:T(8,128)(2,1)S(1)} %get-tuple-element.153.own_ref), channel_id=1, source_target_pairs={{0,1},{1,0},{2,3},{3,2},{4,5},{5,4},{6,7},{7,6},{8,9},{9,8},{10,11... | collective-permute-start | bytes 1572872 | tf_op jit(solution)/shard_map/ppermute | solution.py:597
  31.9 11.3 %copy-start.10 = (bf16[256,256]{1,0:T(8,128)(2,1)S(1)}, bf16[256,256]{1,0:T(8,128)(2,1)}, u32[]{:S(2)}) copy-start(bf16[256,256]{1,0:T(8,128)(2,1)} %constant.35.clone.depth_ref.row_ref) | copy-start | bytes 393220
  31.9 11.3 %copy-start.17 = (bf16[256,256]{1,0:T(8,128)(2,1)S(1)}, bf16[256,256]{1,0:T(8,128)(2,1)}, u32[]{:S(2)}) copy-start(bf16[256,256]{1,0:T(8,128)(2,1)} %constant.34.clone.row_ref.depth_ref) | copy-start | bytes 393220
  43.2 21.8 %copy-start.27 = (bf16[4,8,2,128,128]{4,3,2,1,0:T(8,128)(2,1)S(1)}, bf16[4,8,2,128,128]{4,3,2,1,0:T(8,128)(2,1)}, u32[]{:S(2)}) copy-start(bf16[4,8,2,128,128]{4,3,2,1,0:T(8,128)(2,1)} %get-tuple-element.150.maps_ref) | copy-start | bytes 6291460
  47.3 36.4 %copy-start.6 = (bf16[4,8,256,128]{3,2,1,0:T(8,128)(2,1)}, bf16[4,8,256,128]{3,2,1,0:T(8,128)(2,1)S(1)}, u32[]{:S(2)}) copy-start(bf16[4,8,256,128]{3,2,1,0:T(8,128)(2,1)S(1)} %forward.6.lines_ref) | copy-start | bytes 6291460
  72.4 43.6 %all-to-all-start.4 = ((bf16[16,432,128]{2,1,0:T(8,128)(2,1)}), bf16[16,432,128]{2,1,0:T(8,128)(2,1)}, u32[]{:S(2)}, u32[]{:S(2)}) async-start(bf16[16,432,128]{2,1,0:T(8,128)(2,1)} %get-tuple-element.159), calls=%async_computation.4 | async-start | bytes 3538944 | tf_op jit(solution)/shard_map/all_to_all | solution.py:643
  80.5 25.3 %collective-permute-start.11 = (bf16[8,2,128,128]{3,2,1,0:T(8,128)(2,1)S(1)}, bf16[8,2,128,128]{3,2,1,0:T(8,128)(2,1)S(1)}, u32[]{:S(2)}, u32[]{:S(2)}) collective-permute-start(bf16[8,2,128,128]{3,2,1,0:T(8,128)(2,1)S(1)} %get-tuple-element.162.own_ref), channel_id=1, source_target_pairs={{0,1},{1,0},{2,3},{3,2},{4,5},{5,4},{6,7},{7,6},{8,9},{9,8},{10,11... | collective-permute-start | bytes 1572872 | tf_op jit(solution)/shard_map/ppermute | solution.py:597
  93.8 22.2 %collective-permute-start.12 = (bf16[8,2,128,128]{3,2,1,0:T(8,128)(2,1)}, bf16[8,2,128,128]{3,2,1,0:T(8,128)(2,1)S(1)}, u32[]{:S(2)}, u32[]{:S(2)}) collective-permute-start(bf16[8,2,128,128]{3,2,1,0:T(8,128)(2,1)} %back.19), channel_id=1, source_target_pairs={{0,1},{1,0},{2,3},{3,2},{4,5},{5,4},{6,7},{7,6},{8,9},{9,8},{10,11... | collective-permute-start | bytes 1572872 | tf_op jit(solution)/shard_map/ppermute | solution.py:597
  102.7 16.6 %collective-permute-start.13 = (bf16[8,2,128,128]{3,2,1,0:T(8,128)(2,1)S(1)}, bf16[8,2,128,128]{3,2,1,0:T(8,128)(2,1)}, u32[]{:S(2)}, u32[]{:S(2)}) collective-permute-start(bf16[8,2,128,128]{3,2,1,0:T(8,128)(2,1)S(1)} %back.18), channel_id=1, source_target_pairs={{0,1},{1,0},{2,3},{3,2},{4,5},{5,4},{6,7},{7,6},{8,9},{9,8},{10,11... | collective-permute-start | bytes 1572872 | tf_op jit(solution)/shard_map/ppermute | solution.py:597
  105.8 13.5 %copy-start.12 = (bf16[256,256]{1,0:T(8,128)(2,1)S(1)}, bf16[256,256]{1,0:T(8,128)(2,1)}, u32[]{:S(2)}) copy-start(bf16[256,256]{1,0:T(8,128)(2,1)} %constant.35.clone.depth_ref.row_ref) | copy-start | bytes 393220
  119.3 18.3 %copy-start.13 = (bf16[256,256]{1,0:T(8,128)(2,1)}, bf16[256,256]{1,0:T(8,128)(2,1)S(1)}, u32[]{:S(2)}) copy-start(bf16[256,256]{1,0:T(8,128)(2,1)S(1)} %get-tuple-element.89.row_ref) | copy-start | bytes 393220 | tf_op jit(solution)/shard_map/cond
  119.3 24.6 %all-to-all-start = ((bf16[16,144,128]{2,1,0:T(8,128)(2,1)}), bf16[16,144,128]{2,1,0:T(8,128)(2,1)S(1)}, u32[]{:S(2)}, u32[]{:S(2)}) async-start(bf16[16,144,128]{2,1,0:T(8,128)(2,1)} %get-tuple-element.98), calls=%async_computation | async-start | bytes 1179648 | tf_op jit(solution)/shard_map/cond/branch_0_fun/all_to_all | solution.py:643
  126.0 11.6 %copy-start.9 = (bf16[4,8,256,128]{3,2,1,0:T(8,128)(2,1)S(1)}, bf16[4,8,256,128]{3,2,1,0:T(8,128)(2,1)}, u32[]{:S(2)}) copy-start(bf16[4,8,256,128]{3,2,1,0:T(8,128)(2,1)} %get-tuple-element.102.lines_ref) | copy-start | bytes 6291460 | tf_op jit(solution)/shard_map/cond
  126.0 11.6 %copy-start.19 = (bf16[256,256]{1,0:T(8,128)(2,1)S(1)}, bf16[256,256]{1,0:T(8,128)(2,1)}, u32[]{:S(2)}) copy-start(bf16[256,256]{1,0:T(8,128)(2,1)} %get-tuple-element.88.depth_ref) | copy-start | bytes 393220 | tf_op jit(solution)/shard_map/cond
  126.0 11.6 %copy-start.22 = (f32[4,128,128]{2,1,0:T(8,128)S(1)}, f32[4,128,128]{2,1,0:T(8,128)}, u32[]{:S(2)}) copy-start(f32[4,128,128]{2,1,0:T(8,128)} %get-tuple-element.91.place_ref) | copy-start | bytes 786436 | tf_op jit(solution)/shard_map/cond
  126.0 11.6 %copy-start.25 = (bf16[4,128,128]{2,1,0:T(8,128)(2,1)S(1)}, bf16[4,128,128]{2,1,0:T(8,128)(2,1)}, u32[]{:S(2)}) copy-start(bf16[4,128,128]{2,1,0:T(8,128)(2,1)} %get-tuple-element.92.mask_ref) | copy-start | bytes 393220 | tf_op jit(solution)/shard_map/cond
  126.0 11.6 %copy-start.29 = (bf16[4,8,2,128,128]{4,3,2,1,0:T(8,128)(2,1)S(1)}, bf16[4,8,2,128,128]{4,3,2,1,0:T(8,128)(2,1)}, u32[]{:S(2)}) copy-start(bf16[4,8,2,128,128]{4,3,2,1,0:T(8,128)(2,1)} %get-tuple-element.96.maps_ref) | copy-start | bytes 6291460 | tf_op jit(solution)/shard_map/cond
  126.0 11.6 %copy-start.35 = (f32[8,2,128,128]{3,2,1,0:T(8,128)S(1)}, f32[8,2,128,128]{3,2,1,0:T(8,128)}, u32[]{:S(2)}) copy-start(f32[8,2,128,128]{3,2,1,0:T(8,128)} %get-tuple-element.101.phase_ref) | copy-start | bytes 3145732 | tf_op jit(solution)/shard_map/cond
  136.0 20.4 %collective-permute-start = (bf16[8,2,128,128]{3,2,1,0:T(8,128)(2,1)S(1)}, bf16[8,2,128,128]{3,2,1,0:T(8,128)(2,1)S(1)}, u32[]{:S(2)}, u32[]{:S(2)}) collective-permute-start(bf16[8,2,128,128]{3,2,1,0:T(8,128)(2,1)S(1)} %back.10.rest_2_), channel_id=1, source_target_pairs={{0,1},{1,0},{2,3},{3,2},{4,5},{5,4},{6,7},{7,6},{8,9},{9,8},{10,11... | collective-permute-start | bytes 1572872 | tf_op jit(solution)/shard_map/cond/branch_0_fun/ppermute | solution.py:597
  143.3 13.1 %collective-permute-start.2 = (bf16[4,2,128,128]{3,2,1,0:T(8,128)(2,1)S(1)}, bf16[4,2,128,128]{3,2,1,0:T(8,128)(2,1)S(1)}, u32[]{:S(2)}, u32[]{:S(2)}) collective-permute-start(bf16[4,2,128,128]{3,2,1,0:T(8,128)(2,1)S(1)} %back.11.rest_3_), channel_id=1, source_target_pairs={{0,1},{1,0},{2,3},{3,2},{4,5},{5,4},{6,7},{7,6},{8,9},{9,8},{10,11... | collective-permute-start | bytes 786440 | tf_op jit(solution)/shard_map/cond/branch_0_fun/ppermute | solution.py:597
  150.4 11.1 %collective-permute-start.1 = (bf16[4,2,128,128]{3,2,1,0:T(8,128)(2,1)S(1)}, bf16[4,2,128,128]{3,2,1,0:T(8,128)(2,1)S(1)}, u32[]{:S(2)}, u32[]{:S(2)}) collective-permute-start(bf16[4,2,128,128]{3,2,1,0:T(8,128)(2,1)S(1)} %back.12.rest_3_), channel_id=1, source_target_pairs={{0,1},{1,0},{2,3},{3,2},{4,5},{5,4},{6,7},{7,6},{8,9},{9,8},{10,11... | collective-permute-start | bytes 786440 | tf_op jit(solution)/shard_map/cond/branch_0_fun/ppermute | solution.py:597
  (12 other events, 111.6 us)
